TPU v7x, 256 devices: a whole 4x4x8 slice. The times are simulated.
256 devices in a mesh: dp: 64 (over y, z, core), mix: 4 (over x).
Axes of the slice: x: 4, y: 4, z: 8, core: 2. Of those that a mesh axis runs over, the one named last changes fastest.
Arguments:
- images: bfloat16 [512, 196, 768], P('dp', 'mix'), may hold values from -6 to 6
- cotangent: bfloat16 [512, 196, 768], P('dp', 'mix'), may hold values from -6 to 6
- image_counts: int32 [64], P('dp'), may hold values from 2 to 8, as said below
- w_tok_in: float32 [196, 384], P(None, 'dp'), may hold values from -0.4375 to 0.4375
- w_tok_out: float32 [384, 196], P('dp'), may hold values from -0.3125 to 0.3125
- w_up: float32 [768, 3072], P(None, ('dp', 'mix')), may hold values from -0.21875 to 0.21875
- w_down: float32 [3072, 768], P(('dp', 'mix')), may hold values from -0.109375 to 0.109375
- norm_params: float32 [4, 768], replicated
- biases: float32 [4420], replicated, may hold values from -3 to 3
- left_tok_in: float32 [196, 196], replicated
- right_tok_in: float32 [384, 384], replicated
- left_tok_out: float32 [384, 384], replicated
- right_tok_out: float32 [196, 196], replicated
- left_up: float32 [768, 768], P('dp', 'mix')
- right_up: float32 [3072, 3072], P(None, ('dp', 'mix'))
- left_down: float32 [3072, 3072], P(('dp', 'mix'))
- right_down: float32 [768, 768], P('dp', 'mix')
- root_left_tok_in: float32 [196, 196], replicated
- root_right_tok_in: float32 [384, 384], replicated
- root_left_tok_out: float32 [384, 384], replicated
- root_right_tok_out: float32 [196, 196], replicated
- root_left_up: float32 [768, 768], replicated
- root_right_up: float32 [3072, 3072], P(None, ('dp', 'mix'))
- root_left_down: float32 [3072, 3072], P(('dp', 'mix'))
- root_right_down: float32 [768, 768], replicated
- norm_second: float32 [4, 768], replicated
- bias_second: float32 [4420], replicated
Outputs:
- layer_output: bfloat16 [512, 196, 768], P('dp', 'mix')
- grad_images: float32 [512, 196, 768], P('dp', 'mix')
- grad_tok_in: float32 [196, 384], P(None, 'dp')
- grad_tok_out: float32 [384, 196], P('dp')
- grad_up: float32 [768, 3072], P(None, ('dp', 'mix'))
- grad_down: float32 [3072, 768], P(('dp', 'mix'))
- new_tok_in: float32 [196, 384], P(None, 'dp')
- new_tok_out: float32 [384, 196], P('dp')
- new_up: float32 [768, 3072], P(None, ('dp', 'mix'))
- new_down: float32 [3072, 768], P(('dp', 'mix'))
- new_left_tok_in: float32 [196, 196], replicated
- new_right_tok_in: float32 [384, 384], replicated
- new_left_tok_out: float32 [384, 384], replicated
- new_right_tok_out: float32 [196, 196], replicated
- new_left_up: float32 [768, 768], P('dp', 'mix')
- new_right_up: float32 [3072, 3072], P(None, ('dp', 'mix'))
- new_left_down: float32 [3072, 3072], P(('dp', 'mix'))
- new_right_down: float32 [768, 768], P('dp', 'mix')
- norm_grad: float32 [4, 768], replicated
- norm_second_new: float32 [4, 768], replicated
- norm_new: float32 [4, 768], replicated
- bias_grad: float32 [4420], replicated
- bias_second_new: float32 [4420], replicated
- bias_new: float32 [4420], replicated
Inputs may be any that keep to these rules, and one draw needn't show every extreme that they name: Each index of dp holds 8 image slots; the first image_counts of them hold images and the others are padding. Some index is full in every draw.
All inputs are finite; a program needn't handle non-finite values.
Results may differ from a plain program's by a relative error of at most 0.011.
Values may be sent and summed in bfloat16 or wider, within the bound.
A program may use at most 192 MiB of HBM per device.

v0:
```python
import jax
import jax.numpy as jnp
from jax import lax
from jax.sharding import PartitionSpec as P

DC = 3072
DS = 384
S = 196


HIGH = lax.Precision.HIGHEST
NORM_EPS = 1e-06
DECAY = 0.5
RATE = 0.5
VECTOR_RATE = 0.5
VECTOR_EPS = 1e-08


def layer_norm(values, scale_row, shift_row):
    centre = values - jnp.mean(values, axis=-1, keepdims=True)
    spread = jnp.mean(centre * centre, axis=-1, keepdims=True)
    return centre * lax.rsqrt(spread + NORM_EPS) * scale_row + shift_row


def gelu_exact(values):
    return jax.nn.gelu(values, approximate=False)


def product(left_matrix, right_matrix):
    return jnp.dot(left_matrix, right_matrix, precision=HIGH, preferred_element_type=jnp.float32)


def renew(old_state, left_operand, right_operand, pattern):
    outer = jnp.einsum(
        pattern, left_operand, right_operand, precision=HIGH, preferred_element_type=jnp.float32
    )
    return DECAY * old_state + (1.0 - DECAY) * outer


def take_rows(matrix, offset, length):
    return lax.dynamic_slice_in_dim(matrix, offset, length, 0)


def take_columns(matrix, offset, length):
    return lax.dynamic_slice_in_dim(matrix, offset, length, 1)


def diagonal_step(current, gradient, second):
    new_second = DECAY * second + (1.0 - DECAY) * gradient * gradient
    return (current - VECTOR_RATE * gradient * lax.rsqrt(new_second + VECTOR_EPS), new_second)


def token_forward(channels, tok_in_low, bias_tok_in):
    pre_tok = (
        jnp.einsum("bsc,sk->bck", channels, tok_in_low, preferred_element_type=jnp.float32)
        + bias_tok_in
    )
    return (pre_tok, gelu_exact(pre_tok).astype(jnp.bfloat16))


def on_device(
    images,
    cotangent,
    image_counts,
    w_tok_in,
    w_tok_out,
    w_up,
    w_down,
    norm_params,
    biases,
    left_tok_in,
    right_tok_in,
    left_tok_out,
    right_tok_out,
    left_up,
    right_up,
    left_down,
    right_down,
    root_left_tok_in,
    root_right_tok_in,
    root_left_tok_out,
    root_right_tok_out,
    root_left_up,
    root_right_up,
    root_left_down,
    root_right_down,
    norm_second,
    bias_second,
):
    tok_in_low, tok_out_low = (
        lax.all_gather(w_tok_in.astype(jnp.bfloat16), "dp", axis=1, tiled=True),
        lax.all_gather(w_tok_out.astype(jnp.bfloat16), "dp", axis=0, tiled=True),
    )
    up_low, down_low = (
        lax.all_gather(w_up.astype(jnp.bfloat16), ("dp", "mix"), axis=1, tiled=True),
        lax.all_gather(w_down.astype(jnp.bfloat16), ("dp", "mix"), axis=0, tiled=True),
    )
    bias_tok_in = biases[:DS]
    bias_tok_out = biases[DS : DS + S]
    bias_up = biases[DS + S : DS + S + DC]
    bias_down = biases[DS + S + DC :]
    image_slots = images.shape[0]
    keep_image = (jnp.arange(image_slots) < image_counts[0]).astype(jnp.float32)
    inputs = images.astype(jnp.float32)
    normed = layer_norm(inputs, norm_params[0], norm_params[1]).astype(jnp.bfloat16)
    channels = lax.all_to_all(normed, "mix", split_axis=2, concat_axis=1, tiled=True)
    pre_tok, act_tok = token_forward(channels, tok_in_low, bias_tok_in)
    mixed = (
        jnp.einsum("bck,ks->bsc", act_tok, tok_out_low, preferred_element_type=jnp.float32)
        + bias_tok_out[None, :, None]
    )
    mixed_back = lax.all_to_all(
        mixed.astype(jnp.bfloat16), "mix", split_axis=1, concat_axis=2, tiled=True
    )
    middle = inputs + mixed_back.astype(jnp.float32)
    feature_count = middle.shape[-1]
    middle_flat = middle.reshape(-1, feature_count)
    normed_two = layer_norm(middle_flat, norm_params[2], norm_params[3]).astype(jnp.bfloat16)
    pre_chan = jnp.dot(normed_two, up_low, preferred_element_type=jnp.float32) + bias_up
    act_chan = gelu_exact(pre_chan).astype(jnp.bfloat16)
    branch = jnp.dot(act_chan, down_low, preferred_element_type=jnp.float32) + bias_down
    layer_output = (keep_image[:, None, None] * (middle + branch.reshape(middle.shape))).astype(
        jnp.bfloat16
    )
    masked_back = cotangent * keep_image[:, None, None].astype(jnp.bfloat16)
    back_flat = masked_back.reshape(-1, feature_count)
    down_term = jnp.einsum("nf,nc->fc", act_chan, back_flat, preferred_element_type=jnp.float32)
    bias_down_term = jnp.sum(back_flat.astype(jnp.float32), axis=0)
    d_act_chan = jnp.einsum("nc,fc->nf", back_flat, down_low, preferred_element_type=jnp.float32)
    _, chan_pull = jax.vjp(gelu_exact, pre_chan)
    d_pre_chan = chan_pull(d_act_chan)[0].astype(jnp.bfloat16)
    up_term = jnp.einsum("nc,nf->cf", normed_two, d_pre_chan, preferred_element_type=jnp.float32)
    bias_up_term = jnp.sum(d_pre_chan.astype(jnp.float32), axis=0)
    d_normed_two = jnp.einsum("nf,cf->nc", d_pre_chan, up_low, preferred_element_type=jnp.float32)
    _, second_pull = jax.vjp(layer_norm, middle_flat, norm_params[2], norm_params[3])
    d_middle_norm, gain_two_term, shift_two_term = second_pull(d_normed_two)
    d_middle = masked_back.astype(jnp.float32) + d_middle_norm.reshape(middle.shape)
    d_mixed = lax.all_to_all(
        d_middle.astype(jnp.bfloat16), "mix", split_axis=2, concat_axis=1, tiled=True
    )
    used_channels, used_pre, used_act = (channels, pre_tok, act_tok)
    bias_tok_out_term = jnp.sum(d_mixed.astype(jnp.float32), axis=(0, 2))
    tok_out_term = jnp.einsum("bck,bsc->ks", used_act, d_mixed, preferred_element_type=jnp.float32)
    d_act_tok = jnp.einsum("bsc,ks->bck", d_mixed, tok_out_low, preferred_element_type=jnp.float32)
    _, tok_pull = jax.vjp(gelu_exact, used_pre)
    d_pre_tok = tok_pull(d_act_tok)[0].astype(jnp.bfloat16)
    tok_in_term = jnp.einsum(
        "bsc,bck->sk", used_channels, d_pre_tok, preferred_element_type=jnp.float32
    )
    bias_tok_in_term = jnp.sum(d_pre_tok.astype(jnp.float32), axis=(0, 1))
    d_channels = jnp.einsum(
        "bck,sk->bsc", d_pre_tok, tok_in_low, preferred_element_type=jnp.float32
    ).astype(jnp.bfloat16)
    d_normed = lax.all_to_all(d_channels, "mix", split_axis=1, concat_axis=2, tiled=True)
    _, first_pull = jax.vjp(layer_norm, inputs, norm_params[0], norm_params[1])
    d_inputs, gain_one_term, shift_one_term = first_pull(d_normed.astype(jnp.float32))
    grad_images = d_middle + d_inputs
    norm_term = jnp.stack([gain_one_term, shift_one_term, gain_two_term, shift_two_term])
    bias_term = jnp.concatenate([bias_tok_in_term, bias_tok_out_term, bias_up_term, bias_down_term])
    summed = lax.psum(
        (tok_in_term, tok_out_term, up_term, down_term, norm_term, bias_term), ("dp", "mix")
    )
    per_image = 1.0 / (image_slots * lax.axis_size("dp"))
    grad_tok_in, grad_tok_out, grad_up, grad_down, norm_grad, bias_grad = [
        term * per_image for term in summed
    ]
    dp_index = lax.axis_index("dp")
    mix_index = lax.axis_index("mix")
    flat_index = lax.axis_index(("dp", "mix"))
    tok_in_width = w_tok_in.shape[1]
    tok_in_start = dp_index * tok_in_width
    new_left_tok_in = renew(left_tok_in, grad_tok_in, grad_tok_in, "ik,jk->ij")
    new_right_tok_in = renew(right_tok_in, grad_tok_in, grad_tok_in, "ki,kj->ij")
    step_tok_in = product(
        product(root_left_tok_in, grad_tok_in),
        take_columns(root_right_tok_in, tok_in_start, tok_in_width),
    )
    new_tok_in = w_tok_in - RATE * step_tok_in
    grad_tok_in_part = take_columns(grad_tok_in, tok_in_start, tok_in_width)
    tok_out_rows = w_tok_out.shape[0]
    tok_out_start = dp_index * tok_out_rows
    new_left_tok_out = renew(left_tok_out, grad_tok_out, grad_tok_out, "ik,jk->ij")
    new_right_tok_out = renew(right_tok_out, grad_tok_out, grad_tok_out, "ki,kj->ij")
    step_tok_out = product(
        product(take_rows(root_left_tok_out, tok_out_start, tok_out_rows), grad_tok_out),
        root_right_tok_out,
    )
    new_tok_out = w_tok_out - RATE * step_tok_out
    grad_tok_out_part = take_rows(grad_tok_out, tok_out_start, tok_out_rows)
    up_width = w_up.shape[1]
    up_start = flat_index * up_width
    grad_up_part = take_columns(grad_up, up_start, up_width)
    new_right_up = renew(right_up, grad_up, grad_up_part, "ki,kj->ij")
    up_block_rows, up_block_cols = left_up.shape
    new_left_up = renew(
        left_up,
        take_rows(grad_up, dp_index * up_block_rows, up_block_rows),
        take_rows(grad_up, mix_index * up_block_cols, up_block_cols),
        "ik,jk->ij",
    )
    step_up = product(root_left_up, product(grad_up, root_right_up))
    new_up = w_up - RATE * step_up
    down_rows = w_down.shape[0]
    down_start = flat_index * down_rows
    grad_down_part = take_rows(grad_down, down_start, down_rows)
    new_left_down = renew(left_down, grad_down_part, grad_down, "ik,jk->ij")
    down_block_rows, down_block_cols = right_down.shape
    new_right_down = renew(
        right_down,
        take_columns(grad_down, dp_index * down_block_rows, down_block_rows),
        take_columns(grad_down, mix_index * down_block_cols, down_block_cols),
        "ki,kj->ij",
    )
    step_down = product(product(root_left_down, grad_down), root_right_down)
    new_down = w_down - RATE * step_down
    norm_new, norm_second_new = diagonal_step(norm_params, norm_grad, norm_second)
    bias_new, bias_second_new = diagonal_step(biases, bias_grad, bias_second)
    return (
        layer_output,
        grad_images,
        grad_tok_in_part,
        grad_tok_out_part,
        grad_up_part,
        grad_down_part,
        new_tok_in,
        new_tok_out,
        new_up,
        new_down,
        new_left_tok_in,
        new_right_tok_in,
        new_left_tok_out,
        new_right_tok_out,
        new_left_up,
        new_right_up,
        new_left_down,
        new_right_down,
        norm_grad,
        norm_second_new,
        norm_new,
        bias_grad,
        bias_second_new,
        bias_new,
    )


def solution(mesh):
    in_specs = (
        P("dp", "mix", None),
        P("dp", "mix", None),
        P("dp"),
        P(None, "dp"),
        P("dp", None),
        P(None, ("dp", "mix")),
        P(("dp", "mix"), None),
        P(),
        P(),
        P(),
        P(),
        P(),
        P(),
        P("dp", "mix"),
        P(None, ("dp", "mix")),
        P(("dp", "mix"), None),
        P("dp", "mix"),
        P(),
        P(),
        P(),
        P(),
        P(),
        P(None, ("dp", "mix")),
        P(("dp", "mix"), None),
        P(),
        P(),
        P(),
    )
    out_specs = (
        P("dp", "mix", None),
        P("dp", "mix", None),
        P(None, "dp"),
        P("dp", None),
        P(None, ("dp", "mix")),
        P(("dp", "mix"), None),
        P(None, "dp"),
        P("dp", None),
        P(None, ("dp", "mix")),
        P(("dp", "mix"), None),
        P(),
        P(),
        P(),
        P(),
        P("dp", "mix"),
        P(None, ("dp", "mix")),
        P(("dp", "mix"), None),
        P("dp", "mix"),
        P(),
        P(),
        P(),
        P(),
        P(),
        P(),
    )
    return jax.shard_map(
        on_device, mesh=mesh, in_specs=in_specs, out_specs=out_specs, check_vma=False
    )
```

profile of v0, /device:TPU:1, one launch (start us, length us, event | category | flops | bytes accessed | tf_op | source)
XLA Modules:
  0.0 733.1 jit_solution(16377235715293549956)
XLA Ops:
  17.7 4.5 reshape.201
  22.1 4.8 all-to-all-start
  27.0 48.3 %all-gather.1 = bf16[64,6,196]{2,1,0:T(8,128)(2,1)S(1)} all-gather(bf16[1,6,196]{2,1,0:T(8,128)(2,1)S(1)} %convert_bitcast_fusion.3), channel_id=1, replica_groups=mesh['dp'=64,'mix'=4] {'dp'}, dimensions={0}, use_global_device_ids=true | all-gather | bytes 152880 | tf_op jit(solution)/shard_map/all_gather | solution.py:92
  76.2 43.4 %all-gather = bf16[64,6,196]{2,1,0:T(8,128)(2,1)S(1)} all-gather(bf16[1,6,196]{2,1,0:T(8,128)(2,1)S(1)} %convert_bitcast_fusion.4), channel_id=1, replica_groups=mesh['dp'=64,'mix'=4] {'dp'}, dimensions={0}, use_global_device_ids=true | all-gather | bytes 152880 | tf_op jit(solution)/shard_map/all_gather | solution.py:91
  119.7 5.5 reshape.202
  125.2 4.1 copy.241
  136.5 6.2 multiply_convert_fusion.1
  147.7 5.0 all-to-all-start.1
  159.2 5.9 all-to-all-done.1
  179.8 8.3 %reshape.188 = bf16[3072,768]{1,0:T(8,128)(2,1)} reshape(bf16[256,12,768]{2,1,0:T(8,128)(2,1)} %all-gather.7.cloned.1.call-done) | data formatting | bytes 9437184
  188.2 7.2 fusion.80
  195.4 55.8 %all-gather.9.cloned.1.call-done = bf16[256,12,768]{2,1,0:T(8,128)(2,1)} async-done(((bf16[1,12,768]{2,1,0:T(8,128)(2,1)}), bf16[256,12,768]{2,1,0:T(8,128)(2,1)}) %all-gather.9.cloned.1.call-update) | async-done | bytes 4718608 | tf_op jit(solution)/shard_map/all_gather | solution.py:96
  251.2 8.4 %reshape.190 = bf16[3072,768]{1,0:T(8,128)(2,1)} reshape(bf16[256,12,768]{2,1,0:T(8,128)(2,1)} %all-gather.9.cloned.1.call-done) | data formatting | bytes 9437184
  259.6 15.5 %convert_reduce_fusion = (f32[3072]{0:T(1024)}, bf16[392,3072]{1,0:T(8,128)(2,1)S(1)}, f32[392,3072]{1,0:T(8,128)S(1)}) fusion(f32[392,3072]{1,0:T(8,128)} %fusion.80, f32[3072]{0:T(1024)} %slice.32, bf16[392,768]{1,0:T(8,128)(2,1)} %reshape.175, bf16[3072,768]{1,0:T(8,128)(2,1)} %reshape.190), kind=kOutput, calls=%fused_computation.2 | convolution fusion | flops 1940001792 | bytes 17387520 | tf_op jit(solution)/shard_map/nc,fc->nf/dot_general | solution.py:129
  278.1 5.6 fusion.79
  296.1 4.5 reshape.203
  300.6 4.2 all-to-all-start.2
  304.8 8.1 %fusion.87 = f32[3072,768]{1,0:T(8,128)} fusion(bf16[392,3072]{1,0:T(8,128)(2,1)} %multiply_convert_fusion, bf16[392,768]{1,0:T(8,128)(2,1)} %reshape.175), kind=kOutput, calls=%fused_computation.166 | convolution fusion | flops 1849688064 | bytes 12447744 | tf_op jit(solution)/shard_map/nf,nc->fc/dot_general | solution.py:127
  314.9 6.2 reshape.204
  345.6 4.5 all-to-all-start.3
  350.2 6.2 convolution_add_fusion.2
  377.1 79.0 %all-reduce = (f32[4,768]{1,0:T(4,128)S(1)}, f32[4420]{0:T(1024)S(1)}) all-reduce(f32[4,768]{1,0:T(4,128)S(1)} %pad_maximum_fusion, f32[4420]{0:T(1024)S(1)} %concatenate.3), channel_id=1, replica_groups=mesh['dp'=64,'mix'=4] {'dp','mix'}, use_global_device_ids=true, to_apply=%region_17.0 | all-reduce | flops 7492 | bytes 59936 | tf_op jit(solution)/shard_map/psum | solution.py:160
  457.3 4.5 fusion.35
  461.8 180.3 %all-reduce.4.cloned.1.call-done = (f32[196,384]{1,0:T(8,128)}, f32[384,196]{0,1:T(8,128)}, f32[768,3072]{1,0:T(8,128)}, f32[3072,768]{1,0:T(8,128)}) async-done(((f32[196,384]{1,0:T(8,128)}, f32[384,196]{0,1:T(8,128)}, f32[768,3072]{1,0:T(8,128)}, f32[3072,768]{1,0:T(8,128)}), (f32[196,384]{1,0:T(8,128)}, f32[384,196]{0,1:T(8,128)}, f32[768,3072]{1,0:T(8,128)}, ...) | async-done | bytes 19476496 | tf_op jit(solution)/shard_map/psum | solution.py:160
  642.1 9.2 %broadcast_multiply_fusion.1 = f32[768,3072]{1,0:T(8,128)} fusion(f32[768,3072]{1,0:T(8,128)} %get-tuple-element.207), kind=kLoop, calls=%fused_computation.19 | loop fusion | flops 2359296 | bytes 18874368 | tf_op jit(solution)/shard_map/mul | solution.py:165
  651.3 10.6 %fusion.81 = f32[768,12]{0,1:T(8,128)S(1)} fusion(f32[3072,12]{0,1:T(8,128)S(1)} %copy-done.24, f32[768,3072]{1,0:T(8,128)} %get-tuple-element.207), kind=kOutput, calls=%fused_computation.162 | convolution fusion | flops 342097920 | bytes 9621504 | tf_op jit(solution)/shard_map/dot_general | solution.py:30
  662.0 4.2 broadcast_multiply_fusion
  666.2 5.1 fusion.82
  687.1 9.9 %fusion.7 = f32[3072,12]{0,1:T(8,128)} fusion(f32[3072,12]{0,1:T(8,128)S(1)} %copy-done.26, f32[768,12]{1,0:T(8,128)S(1)} %constant_dynamic-slice_fusion.1, f32[768,3072]{1,0:T(8,128)} %get-tuple-element.207), kind=kOutput, calls=%fused_computation.24 | convolution fusion | flops 342171648 | bytes 9768960 | tf_op jit(solution)/shard_map/ki,kj->ij/dot_general | solution.py:34
  697.9 4.3 fusion.44
  702.3 7.9 %fusion.57 = f32[12,192]{1,0:T(8,128)} fusion(f32[12,192]{1,0:T(8,128)S(1)} %copy-done.38, f32[3072,768]{1,0:T(8,128)} %broadcast_multiply_fusion, s32[]{:T(128)S(6)} %select_n.21, s32[]{:T(128)S(6)} %select_n.20), kind=kOutput, calls=%fused_computation.110 | convolution fusion | flops 84939264 | bytes 4737032 | tf_op jit(solution)/shard_map/ki,kj->ij/dot_general | solution.py:34
  717.7 8.5 %fusion.6 = f32[12,3072]{1,0:T(8,128)} fusion(f32[12,3072]{1,0:T(8,128)S(1)} %copy-done.27, f32[12,768]{1,0:T(8,128)S(1)} %constant_dynamic-slice_fusion, f32[3072,768]{1,0:T(8,128)S(1)} %bitcast.98), kind=kOutput, calls=%fused_computation.22 | convolution fusion | flops 342171648 | bytes 9768960 | tf_op jit(solution)/shard_map/ik,jk->ij/dot_general | solution.py:34
  (254 shorter events, 131.9 us)
Async XLA Ops:
  7.2 703.8 %copy-start = (f32[768,768]{1,0:T(8,128)S(1)}, f32[768,768]{1,0:T(8,128)}, u32[]{:S(2)}) copy-start(f32[768,768]{1,0:T(8,128)} %param.48) | copy-start | bytes 7077892
  7.2 172.6 %all-gather.7.cloned.1.call-start = ((), (), s32[]{:S(2)}) async-start(), calls=%async_computation.4 | async-start | bytes 6316032 | tf_op jit(solution)/shard_map/all_gather | solution.py:95
  8.8 242.3 %all-gather.9.cloned.1.call-start = ((), (), s32[]{:S(2)}) async-start(), calls=%async_computation.5 | async-start | bytes 6316032 | tf_op jit(solution)/shard_map/all_gather | solution.py:96
  14.2 174.0 %copy-start.40 = (f32[768]{0:T(1024)}, f32[768]{0:T(1024)S(1)}, u32[]{:S(2)}) copy-start(f32[768]{0:T(1024)S(1)} %get-tuple-element.199) | copy-start | bytes 9220
  14.2 174.0 %copy-start.51 = (f32[768]{0:T(1024)}, f32[768]{0:T(1024)S(1)}, u32[]{:S(2)}) copy-start(f32[768]{0:T(1024)S(1)} %get-tuple-element.202) | copy-start | bytes 9220
  15.6 11.4 %copy-start.28 = (f32[4420]{0:T(1024)S(1)}, f32[4420]{0:T(1024)}, u32[]{:S(2)}) copy-start(f32[4420]{0:T(1024)} %param.35) | copy-start | bytes 53044
  15.6 11.4 %copy-start.34 = (f32[6,196]{1,0:T(8,128)S(1)}, f32[6,196]{1,0:T(8,128)}, u32[]{:S(2)}) copy-start(f32[6,196]{1,0:T(8,128)} %param.31) | copy-start | bytes 14116
  17.7 58.5 %copy-start.32 = (f32[196,6]{0,1:T(8,128)S(1)}, f32[196,6]{0,1:T(8,128)}, u32[]{:S(2)}) copy-start(f32[196,6]{0,1:T(8,128)} %param.30) | copy-start | bytes 14116
  22.1 97.6 %all-to-all-start = ((bf16[4,2,37632]{2,1,0:T(2,128)(2,1)}), bf16[4,2,37632]{2,1,0:T(2,128)(2,1)S(1)}, u32[]{:S(2)}, u32[]{:S(2)}) async-start(bf16[4,2,37632]{2,1,0:T(2,128)(2,1)} %reshape.201), calls=%async_computation | async-start | bytes 1204224 | tf_op jit(solution)/shard_map/all_to_all | solution.py:106
  27.0 109.4 %copy-start.47 = (f32[384]{0:T(512)}, f32[384]{0:T(512)S(1)}, u32[]{:S(2)}) copy-start(f32[384]{0:T(512)S(1)} %slice.28) | copy-start | bytes 4612
  119.7 14.5 %copy-start.13 = (bf16[384,196]{1,0:T(8,128)(2,1)}, bf16[384,196]{1,0:T(8,128)(2,1)S(1)}, u32[]{:S(2)}) copy-start(bf16[384,196]{1,0:T(8,128)(2,1)S(1)} %reshape.184) | copy-start | bytes 451588
  147.7 17.4 %all-to-all-start.1 = ((bf16[8,196,192]{2,0,1:T(8,128)(2,1)}), bf16[8,196,192]{2,0,1:T(8,128)(2,1)}, u32[]{:S(2)}, u32[]{:S(2)}) async-start(bf16[8,196,192]{2,0,1:T(8,128)(2,1)} %copy.208), calls=%async_computation.1 | async-start | bytes 1605632 | tf_op jit(solution)/shard_map/all_to_all | solution.py:112
  173.8 14.4 %copy-start.45 = (f32[392]{0:T(512)}, f32[392]{0:T(512)S(1)}, u32[]{:S(2)}) copy-start(f32[392]{0:T(512)S(1)} %div.45) | copy-start | bytes 4708
  251.2 24.0 %slice-start.8 = ((s8[4718592]{0:T(1024)(128)(4,1)}), s8[524288]{0:T(1024)(128)(4,1)S(1)}, s32[]{:S(2)}) async-start(s8[4718592]{0:T(1024)(128)(4,1)} %bitcast.107), calls=%async_computation.15 | async-start | bytes 1048576
  259.6 15.6 %copy-start.6 = (f32[392,768]{1,0:T(8,128)S(1)}, f32[392,768]{1,0:T(8,128)}, u32[]{:S(2)}) copy-start(f32[392,768]{1,0:T(8,128)} %reshape.173) | copy-start | bytes 3612676
  259.6 15.6 %slice-start.9 = ((s8[4718592]{0:T(1024)(128)(4,1)}), s8[4194304]{0:T(1024)(128)(4,1)S(1)}, s32[]{:S(2)}) async-start(s8[4718592]{0:T(1024)(128)(4,1)} %bitcast.107), calls=%async_computation.16 | async-start | bytes 8388608
  259.6 15.6 %copy-start.41 = (f32[768]{0:T(1024)S(1)}, f32[768]{0:T(1024)}, u32[]{:S(2)}) copy-start(f32[768]{0:T(1024)} %copy-done.40) | copy-start | bytes 9220
  259.6 15.6 %copy-start.46 = (f32[392]{0:T(512)S(1)}, f32[392]{0:T(512)}, u32[]{:S(2)}) copy-start(f32[392]{0:T(512)} %copy-done.45) | copy-start | bytes 4708
  259.6 15.6 %copy-start.50 = (f32[392]{0:T(512)S(1)}, f32[392]{0:T(512)}, u32[]{:S(2)}) copy-start(f32[392]{0:T(512)} %copy-done.49) | copy-start | bytes 4708
  300.6 14.3 %all-to-all-start.2 = ((bf16[4,2,37632]{2,1,0:T(2,128)(2,1)}), bf16[4,2,37632]{2,1,0:T(2,128)(2,1)}, u32[]{:S(2)}, u32[]{:S(2)}) async-start(bf16[4,2,37632]{2,1,0:T(2,128)(2,1)} %reshape.203), calls=%async_computation.2 | async-start | bytes 1204224 | tf_op jit(solution)/shard_map/all_to_all | solution.py:138
  304.7 337.4 %all-reduce.4.cloned.1.call-start = ((), (), s32[]{:S(2)}) async-start(), calls=%async_computation.6 | async-start | bytes 38977536 | tf_op jit(solution)/shard_map/psum | solution.py:160
  345.6 19.2 %all-to-all-start.3 = ((bf16[8,196,192]{2,0,1:T(8,128)(2,1)}), bf16[8,196,192]{2,0,1:T(8,128)(2,1)}, u32[]{:S(2)}, u32[]{:S(2)}) async-start(bf16[8,196,192]{2,0,1:T(8,128)(2,1)} %copy.223), calls=%async_computation.3 | async-start | bytes 1605632 | tf_op jit(solution)/shard_map/all_to_all | solution.py:154
  373.0 83.1 %copy-start.31 = (f32[4,768]{1,0:T(4,128)S(1)}, f32[4,768]{1,0:T(4,128)}, u32[]{:S(2)}) copy-start(f32[4,768]{1,0:T(4,128)} %param.34) | copy-start | bytes 36868
  373.0 83.1 %copy-start.42 = (f32[4,768]{1,0:T(4,128)S(1)}, f32[4,768]{1,0:T(4,128)}, u32[]{:S(2)}) copy-start(f32[4,768]{1,0:T(4,128)} %param.52) | copy-start | bytes 36868
  373.0 83.7 %copy-start.36 = (f32[4420]{0:T(1024)S(1)}, f32[4420]{0:T(1024)}, u32[]{:S(2)}) copy-start(f32[4420]{0:T(1024)} %param.53) | copy-start | bytes 53044
  373.0 84.3 %copy-start.55 = (f32[8]{0:T(128)S(1)}, f32[8]{0:T(128)}, u32[]{:S(2)}) copy-start(f32[8]{0:T(128)} %compare_convert_fusion) | copy-start | bytes 100
  642.1 19.8 %slice-start = ((s8[9437184]{0:T(1024)(128)(4,1)}), s8[4194304]{0:T(1024)(128)(4,1)S(1)}, s32[]{:S(2)}) async-start(s8[9437184]{0:T(1024)(128)(4,1)} %bitcast.95), calls=%async_computation.7 | async-start | bytes 8388608
  642.1 19.8 %slice-start.1 = ((s8[9437184]{0:T(1024)(128)(4,1)}), s8[4194304]{0:T(1024)(128)(4,1)S(1)}, s32[]{:S(2)}) async-start(s8[9437184]{0:T(1024)(128)(4,1)} %bitcast.95), calls=%async_computation.8 | async-start | bytes 8388608
  687.1 30.6 %slice-start.3 = ((s8[9437184]{0:T(1024)(128)(4,1)}), s8[4194304]{0:T(1024)(128)(4,1)S(1)}, s32[]{:S(2)}) async-start(s8[9437184]{0:T(1024)(128)(4,1)} %bitcast.97), calls=%async_computation.10 | async-start | bytes 8388608
  687.1 30.6 %slice-start.4 = ((s8[9437184]{0:T(1024)(128)(4,1)}), s8[4194304]{0:T(1024)(128)(4,1)S(1)}, s32[]{:S(2)}) async-start(s8[9437184]{0:T(1024)(128)(4,1)} %bitcast.97), calls=%async_computation.11 | async-start | bytes 8388608
  697.9 19.8 %copy-start.19 = (f32[12,768]{1,0:T(8,128)}, f32[12,768]{1,0:T(8,128)S(1)}, u32[]{:S(2)}) copy-start(f32[12,768]{1,0:T(8,128)S(1)} %constant_dynamic-slice_fusion) | copy-start | bytes 110596
  702.3 15.5 %slice-start.5 = ((s8[9437184]{0:T(1024)(128)(4,1)}), s8[1048576]{0:T(1024)(128)(4,1)S(1)}, s32[]{:S(2)}) async-start(s8[9437184]{0:T(1024)(128)(4,1)} %bitcast.97), calls=%async_computation.12 | async-start | bytes 2097152
  (41 other events, 242.1 us)
Sparse Core Ops, SparseCore 0:
  12.5 120.4 all-gather.6
  137.4 113.7 all-gather.8
  339.2 302.8 all-reduce.3
where the time goes:
time: 740 us; the launch traced here: 733 us
  waiting for transfers between devices  248 us (34%)
  blocking collectives  171 us (23%)
  matrix products  124 us (17%)
  local copies, waits for them, and re-layouts  102 us (14%)
  other arithmetic  54.6 us (7%)
  starting transfers between devices  18.7 us (3%)
  between operations  15.4 us (2%)
    psum x1, waiting for transfers between devices, on_device(): lax.psum((tok_in_term, tok_out_term, up_term, down_term, norm_term, bias_...  180 us
    psum x1, blocking collectives, on_device(): lax.psum((tok_in_term, tok_out_term, up_term, down_term, norm_term, bias_...  79 us
    all_gather x1, waiting for transfers between devices, on_device(): lax.all_gather(w_down.astype(jnp.bfloat16), ('dp', 'mix'), axis=0, tiled=...  55.8 us
    all_gather x1, blocking collectives, on_device(): lax.all_gather(w_tok_out.astype(jnp.bfloat16), 'dp', axis=0, tiled=True)  48.3 us
    unnamed x143, local copies, waits for them, and re-layouts  43.5 us
    all_gather x1, blocking collectives, on_device(): lax.all_gather(w_tok_in.astype(jnp.bfloat16), 'dp', axis=1, tiled=True)  43.4 us
    dot_general x8, matrix products, renew(): jnp.einsum(pattern, left_operand, right_operand, precision=HIGH, preferre...  38.6 us
    dot_general x8, matrix products, product(): jnp.dot(left_matrix, right_matrix, precision=HIGH, preferred_element_type...  25.6 us
  transfers between devices with their start and end apart: 7, of which 5 were waited for; matrix products, arithmetic and copies ran while one was open for 16% of the time, Pallas kernels for 0%

commit v1 on v0

v1 whole, which is shorter than its diff:
```python
import jax
import jax.numpy as jnp
from jax import lax
from jax.experimental import pallas as pl
from jax.experimental.pallas import tpu as pltpu
from jax.sharding import PartitionSpec as P

MESH = pl.DeviceIdType.MESH
BF = jnp.bfloat16
F32 = jnp.float32
HIGH = lax.Precision.HIGHEST

D = 768
DC = 3072
DS = 384
S = 196
NX, NY, NZ = 4, 4, 8
EPS = 1e-06
PER_IMAGE = 1.0 / 512.0
PATCHES = 49
PAIR = 112
IMG = 256
ROW = 208
HALF = D // 2
LANES = (slice(0, HALF), slice(HALF, D))


def dot(left, right, left_dim=1, right_dim=0, precision=None):
    return lax.dot_general(
        left,
        right,
        (((left_dim,), (right_dim,)), ((), ())),
        preferred_element_type=F32,
        precision=precision,
    )


def pick(rows, cols, rule):
    row = lax.broadcasted_iota(jnp.int32, (rows, cols), 0)
    col = lax.broadcasted_iota(jnp.int32, (rows, cols), 1)
    return jnp.where(rule(row, col), 1.0, 0.0).astype(BF)


def ge(values, bound):
    return (values >= bound).astype(jnp.int32)


def gelu_and_slope(v):
    t = pl.reciprocal(1.0 + 0.23164188 * jnp.abs(v))
    e = jnp.exp(-0.5 * v * v)
    q = 0.5 * t * (
        0.254829592 + t * (-0.284496736 + t * (1.421413741 + t * (-1.453152027 + t * 1.061405429)))
    ) * e
    cdf = jnp.where(v >= 0, 1.0 - q, q)
    return v * cdf, cdf + v * e * 0.3989422804014327


def normalise(v):
    mean = jnp.mean(v, axis=-1, keepdims=True)
    centre = v - mean
    r = lax.rsqrt(jnp.mean(centre * centre, axis=-1, keepdims=True) + EPS)
    return centre * r, r


def normalise_back(xhat, r, dh, gain):
    dxh = dh * gain
    m1 = jnp.mean(dxh, axis=-1, keepdims=True)
    m2 = jnp.mean(dxh * xhat, axis=-1, keepdims=True)
    dv = r * (dxh - m1 - xhat * m2)
    return dv, jnp.sum(dh * xhat, axis=0, keepdims=True), jnp.sum(dh, axis=0, keepdims=True)


def fused(
    count, img, cot, tin, tout, wup, wdn, norm, btin, btout, bup, bdn,
    q_up, p_dn, p_up, q_dn, old_r_up, old_l_dn, old_l_up, old_r_dn,
    pl_ti, pr_ti, pl_to, pr_to, ol_ti, or_ti, ol_to, or_to,
    o_layer, o_gimg, o_gup, o_gdn, o_nup, o_ndn, o_rup, o_ldn, o_lup, o_rdn,
    o_small, o_gti, o_gto, o_nti, o_nto, o_lti, o_rti, o_lto, o_rto,
    ssem, rsem, lsem, stage, wst, tst, simg, scot, rimg, rcot, rlay, rgrad,
    xw, W, tk, tokin, tokout, ximg, normed, mid, slope, act, n2, mb, br, dn,
    upc, dnc, actb, dpb, xbi, G, RAr, RAl, XA, XB, RBr, RBl, PY,
    UJ, UJP, H, qst, Qx, XEo, XEi, SM, SB, SRr, SRl, SX, SY, SC, SF,
):
    dp = lax.axis_index("dp")
    x = lax.axis_index("mix")
    c = lax.rem(dp, 2)
    y = dp // (2 * NZ)
    z = lax.rem(dp // 2, NZ)

    def X(i):
        return lax.rem(x + i + NX, NX)

    def Y(i):
        return lax.rem(y + i + NY, NY)

    def Z(i):
        return lax.rem(z + i + NZ, NZ)

    def dev(xx, yy, zz, cc):
        return ((yy * NZ + zz) * 2 + cc, xx)

    to_x = [None] + [dev(X(i), y, z, c) for i in range(1, NX)]
    to_y = [None] + [dev(x, Y(i), z, c) for i in range(1, NY)]
    to_z = [None] + [dev(x, y, Z(i), c) for i in range(1, NZ)]
    sibling = dev(x, y, z, 1 - c)
    started = []
    used = [0]

    def put(src, dst, device):
        k = used[0]
        used[0] += 1
        copy = pltpu.make_async_remote_copy(
            src_ref=src, dst_ref=dst, send_sem=ssem.at[k], recv_sem=rsem.at[k],
            device_id=device, device_id_type=MESH,
        )
        copy.start()
        started.append(copy)
        return copy

    def arrived(copies):
        for copy in copies:
            copy.wait_recv()

    def total(*parts):
        value = parts[0].astype(F32)
        for part in parts[1:]:
            value = value + part.astype(F32)
        return value

    stage[...] = jnp.zeros_like(stage)
    stage[0:12, 0:D] = wup[...]
    stage[16:28, 0:D] = wdn[...]
    stage[0:6, D : D + S] = tin[...]
    stage[8:14, D : D + S] = tout[...]
    wst[...] = stage[:, 0:D].astype(BF)
    tst[...] = stage[0:16, D : D + 256].astype(BF)
    xw[x] = wst[...]
    tk[y, z, c] = tst[...]
    stage[0:12, :] = q_up[...]
    stage[12:16, :] = jnp.zeros((4, DC), F32)
    stage[16:28, :] = p_dn[...]
    qst[0] = stage[0:16, :].astype(BF)
    qst[1] = stage[16:32, :].astype(BF)
    Qx[:, x] = qst[:, :, pl.ds(pl.multiple_of(x * D, D), D)]
    for m in range(NX):
        def of_pair(row, col, m=m):
            second = ge(row, PATCHES)
            return (col == (row - PATCHES * second) * 8 + 2 * m + second) & (row < 2 * PATCHES)

        chooser = pick(PAIR, 8 * PATCHES, of_pair)
        simg[m] = dot(chooser, img[...]).astype(BF)
        scot[m] = dot(chooser, cot[...]).astype(BF)
    rimg[x] = simg[x]
    rcot[x] = scot[x]

    barrier = pltpu.get_barrier_semaphore()
    peers = to_x[1:] + to_y[1:] + to_z[1:] + [sibling]
    for peer in peers:
        pl.semaphore_signal(barrier, inc=1, device_id=peer, device_id_type=MESH)
    pl.semaphore_wait(barrier, len(peers))

    c_xw = [put(wst, xw.at[x], to_x[i]) for i in range(1, NX)]
    c_ty = [put(tk.at[y, z, c], tk.at[y, z, c], to_y[i]) for i in range(1, NY)]
    c_img = [put(simg.at[X(i)], rimg.at[x], to_x[i]) for i in range(1, NX)]

    arrived(c_xw)

    def of_shards(row, col):
        m, j = col >> 5, col & 31
        up = (j < 12) & (row == 12 * m + j)
        down = (j >= 16) & (j < 28) & (row == 32 + 12 * m + j)
        return up | down

    W[y, z] = dot(pick(96, 128, of_shards), xw[...].reshape(128, D)).astype(BF)

    LA, LB = LANES
    a_right, a_left, b_right, b_left, b_y = {}, {}, {}, {}, {}

    def a_send(step, d, right):
        if right:
            ref = W.at[Y(-d), Z(1 - step), :, LA]
            a_right[step, d] = put(ref, ref, to_z[1])
        else:
            ref = W.at[Y(-d), Z(step - 1), :, LA]
            a_left[step, d] = put(ref, ref, to_z[7])

    def b_send(step, right):
        if right:
            ref = W.at[y, Z(1 - step), :, LB]
            b_right[step] = put(ref, ref, to_z[1])
        else:
            ref = W.at[y, Z(step - 1), :, LB]
            b_left[step] = put(ref, ref, to_z[7])

    def b_spread(offset):
        ref = W.at[y, Z(offset), :, LB]
        b_y[offset] = [put(ref, ref, to_y[i]) for i in range(1, NY)]

    b_send(1, True)
    b_send(1, False)
    own_a = W.at[y, z, :, LA]
    c_ay = [None] + [put(own_a, own_a, to_y[i]) for i in range(1, NY)]
    a_send(1, 0, True)
    a_send(1, 0, False)
    b_spread(0)
    arrived(c_ty)
    c_tz = [put(tk.at[:, z, c], tk.at[:, z, c], to_z[i]) for i in range(1, NZ)]
    c_cot = [put(scot.at[X(i)], rcot.at[x], to_x[i]) for i in range(1, NX)]
    c_q = [
        put(qst.at[:, :, pl.ds(pl.multiple_of(X(i) * D, D), D)], Qx.at[:, x], to_x[i])
        for i in range(1, NX)
    ]
    for d in (1, 3, 2):
        c_ay[d].wait_recv()
        a_send(1, d, True)
        a_send(1, d, False)

    def gather_step(step):
        b_right[step].wait_recv()
        if step < 4:
            b_send(step + 1, True)
        b_spread(-step)
        if step < 4:
            b_left[step].wait_recv()
            if step < 3:
                b_send(step + 1, False)
            b_spread(step)
        for d in (0, 1, 3, 2):
            a_right[step, d].wait_recv()
            if step < 4:
                a_send(step + 1, d, True)
                a_left[step, d].wait_recv()
                if step < 3:
                    a_send(step + 1, d, False)

    arrived(c_tz)
    c_tc = put(tk.at[:, :, c], tk.at[:, :, c], sibling)
    gather_step(1)
    c_tc.wait_recv()

    def of_group(row, col):
        group, i = col >> 4, col & 15
        first = (i < 6) & (row == 6 * group + i)
        second = (i >= 8) & (i < 14) & (row == 40 + 6 * group + i)
        return first | second

    chooser = pick(96, 128, of_group)
    for g in range(8):
        part = tk[g // 2, 4 * (g % 2) : 4 * (g % 2) + 4].reshape(128, 256)
        part = dot(chooser, part).astype(BF)
        tokin[48 * g : 48 * g + 48, :] = part[0:48]
        tokout[48 * g : 48 * g + 48, :] = part[48:96]

    arrived(c_img)
    arrived(c_cot)
    keep = [jnp.where(2 * x + b < count[0], 1.0, 0.0).astype(F32) for b in range(2)]
    own = c * (2 * ROW)

    def own_rows(b):
        return pl.ds(pl.multiple_of(own + b * ROW, 16), ROW)

    both = pl.ds(pl.multiple_of(own, 16), 2 * ROW)
    for b in range(2):
        def of_image(row, col, b=b):
            part = ge(row, 49) + ge(row, 98) + ge(row, 147)
            return (col == 63 * part + 49 * b + row) & (row < S)

        chooser = pick(IMG, NX * PAIR, of_image)
        pixels = dot(chooser, rimg[...].reshape(NX * PAIR, D))
        ximg[b] = pixels
        back = dot(chooser[0:ROW], rcot[...].reshape(NX * PAIR, D)) * keep[b]
        mb[own_rows(b), :] = back.astype(BF)
        xhat, _ = normalise(pixels)
        normed[b] = (xhat * norm[0:1, :] + norm[1:2, :]).astype(BF)
    c_mb = put(mb.at[both], mb.at[both], sibling)
    gather_step(2)

    @pl.loop(0, 2)
    def _(b):
        pre = dot(tokin[...], normed[b]) + btin[...]
        value, grad = gelu_and_slope(pre)
        slope[b] = grad
        act[b] = value.astype(BF)
        mixed = dot(tokout[...], act[b], 0, 0) + btout[...]
        middle = ximg[b] + mixed.astype(BF).astype(F32)
        mid[b] = middle
        xhat, _ = normalise(middle[0:ROW])
        n2[own_rows(b), :] = (xhat * norm[2:3, :] + norm[3:4, :]).astype(BF)

    c_n2 = put(n2.at[both], n2.at[both], sibling)
    gather_step(3)
    gather_step(4)
    for offset in (0, -1, 1, -2, 2, -3, 3, -4):
        arrived(b_y[offset])
    c_mb.wait_recv()
    c_n2.wait_recv()

    SM[...] = jnp.zeros_like(SM)
    br[...] = jnp.zeros_like(br)
    dn[...] = jnp.zeros_like(dn)

    @pl.loop(0, 2)
    def _(half):
        for j in range(4):
            zz = Z(4 * half + j)
            upc[192 * j : 192 * j + 192, :] = W[:, zz, 0:48, :].reshape(192, D)
            dnc[192 * j : 192 * j + 192, :] = W[:, zz, 48:96, :].reshape(192, D)
        bias = jnp.concatenate([bup[2 * Z(4 * half + j) + c] for j in range(4)], axis=1)

        @pl.loop(0, 4)
        def _(r):
            rows = pl.ds(pl.multiple_of(r * ROW, 16), ROW)
            pre = dot(n2[rows, :], upc[...], 1, 1) + bias
            value, grad = gelu_and_slope(pre)
            low = value.astype(BF)
            actb[rows, :] = low
            br[rows, :] += dot(low, dnc[...])
            low = (grad * dot(mb[rows, :], dnc[...], 1, 1)).astype(BF)
            dpb[rows, :] = low
            dn[rows, :] += dot(low, upc[...])

        sums = dot(jnp.ones((8, 4 * ROW), BF), dpb[...])[0:1]
        for h in range(2):
            lanes = slice(384 * h, 384 * h + 384)
            for u, (left, right) in enumerate(((dpb, n2), (actb, mb))):
                grad = dot(left[:, lanes], right[...], 0, 0).astype(BF)
                for j in range(2):
                    part = grad[192 * j : 192 * j + 192].reshape(4, 48, D)
                    G[:, Z(4 * half + 2 * h + j), 48 * u : 48 * u + 48, :] = part
        for j in range(4):
            SM[pl.ds(464 + 8 * c + Z(4 * half + j), 1), 0:192] = sums[:, 192 * j : 192 * j + 192]

    other = pl.ds(pl.multiple_of((1 - c) * (2 * ROW), 16), 2 * ROW)
    upc[0 : 2 * ROW, :] = dn[other, :].astype(BF)
    c_dn = put(upc.at[0 : 2 * ROW], xbi.at[1], sibling)
    dnc[0 : 2 * ROW, :] = br[other, :].astype(BF)
    c_br = put(dnc.at[0 : 2 * ROW], xbi.at[0], sibling)

    ra, la, rb, lb, xb = {}, {}, {}, {}, {}

    def a_reduce(step):
        for w in range(NX):
            ref = G.at[X(w), Z(5 - step), :, LA]
            if step > 1:
                ra[step - 1, w].wait_recv()
                ref[...] = total(ref[...], RAr[step - 2, w]).astype(BF)
            ra[step, w] = put(ref, RAr.at[step - 1, w], to_z[1])
            if step < 4:
                ref = G.at[X(w), Z(step - 4), :, LA]
                if step > 1:
                    la[step - 1, w].wait_recv()
                    ref[...] = total(ref[...], RAl[step - 2, w]).astype(BF)
                la[step, w] = put(ref, RAl.at[step - 1, w], to_z[7])

    def b_sum(k, extra):
        arrived([xb[k % 8, i] for i in range(1, NX)])
        ref = G.at[x, Z(k), :, LB]
        parts = [XB[i, Z(k)] for i in range(NX - 1)]
        ref[...] = total(ref[...], *parts, *extra).astype(BF)
        return ref

    def b_reduce(step):
        extra = []
        if step > 1:
            rb[step - 1].wait_recv()
            extra = [RBr[step - 2]]
        rb[step] = put(b_sum(5 - step, extra), RBr.at[step - 1], to_z[1])
        if step < 4:
            extra = []
            if step > 1:
                lb[step - 1].wait_recv()
                extra = [RBl[step - 2]]
            lb[step] = put(b_sum(step - 4, extra), RBl.at[step - 1], to_z[7])

    a_reduce(1)
    for k in (4, 5, 3, 6, 2, 7, 1, 0):
        for i in range(1, NX):
            xb[k, i] = put(G.at[X(i), Z(k), :, LB], XB.at[i - 1, Z(k)], to_x[i])

    c_dn.wait_recv()
    c_br.wait_recv()
    lob, dmx = actb, dpb
    lob[0 : 2 * IMG, :] = jnp.zeros((2 * IMG, D), BF)
    dmx[0 : 2 * IMG, :] = jnp.zeros((2 * IMG, D), BF)
    gain_two = jnp.zeros((1, D), F32)
    shift_two = jnp.zeros((1, D), F32)
    for b in range(2):
        here = slice(b * ROW, b * ROW + ROW)
        branch = br[own_rows(b), :] + xbi[0, here, :].astype(F32) + bdn[...]
        lob[b * IMG : b * IMG + ROW, :] = (keep[b] * (mid[b, 0:ROW] + branch)).astype(BF)
        dh = dn[own_rows(b), :] + xbi[1, here, :].astype(F32)
        xhat, r = normalise(mid[b, 0:ROW])
        dv, gain, shift = normalise_back(xhat, r, dh, norm[2:3, :])
        gain_two = gain_two + gain
        shift_two = shift_two + shift
        back = mb[own_rows(b), :].astype(F32) + dv
        mid[b, 0:ROW] = back
        dmx[b * IMG : b * IMG + ROW, :] = back.astype(BF)

    def out_rows(m):
        def of_out(row, col):
            second = ge(row, PATCHES)
            place = (IMG - PATCHES) * second + PATCHES * m + row
            return (col == place) & (row < 2 * PATCHES)

        return pick(PAIR, 2 * IMG, of_out)

    a_reduce(2)
    for copy in c_img:
        copy.wait_send()
    for m in range(NX):
        simg[m] = dot(out_rows(m), lob[0 : 2 * IMG, :]).astype(BF)
    rlay[x] = simg[x]
    c_lay = [put(simg.at[X(i)], rlay.at[x], to_x[i]) for i in range(1, NX)]

    roots = [
        pltpu.make_async_copy(p_up, br.at[0:D], lsem.at[0]),
        pltpu.make_async_copy(q_dn, dn.at[0:D], lsem.at[1]),
    ]
    for copy in roots:
        copy.start()
    gti = jnp.zeros((IMG, DS), F32)
    gto = jnp.zeros((IMG, DS), F32)
    bti = jnp.zeros((8, DS), F32)
    bto = jnp.zeros((8, IMG), F32)
    gain_one = jnp.zeros((1, D), F32)
    shift_one = jnp.zeros((1, D), F32)
    ones = jnp.ones((8, D), BF)
    for b in range(2):
        dmixed = dmx[b * IMG : b * IMG + IMG, :]
        dpre = (slope[b] * dot(tokout[...], dmixed)).astype(BF)
        gti = gti + dot(normed[b], dpre, 1, 1)
        gto = gto + dot(dmixed, act[b], 1, 1)
        bti = bti + dot(ones, dpre, 1, 1)
        bto = bto + dot(ones, dmixed, 1, 1)
        dnormed = dot(tokin[...], dpre, 0, 0).astype(BF).astype(F32)
        xhat, r = normalise(ximg[b, 0:ROW])
        dv, gain, shift = normalise_back(xhat, r, dnormed[0:ROW], norm[0:1, :])
        gain_one = gain_one + gain
        shift_one = shift_one + shift
        lob[b * IMG : b * IMG + ROW, :] = (mid[b, 0:ROW] + dv).astype(BF)
        a_reduce(3 + b)

    SM[0:IMG, :] = gti
    SM[IMG : IMG + ROW, :] = gto[0:ROW]
    for j, row in enumerate((gain_one, shift_one, gain_two, shift_two)):
        SM[208 + 2 * j : 209 + 2 * j, :] = row[:, 0:HALF]
        SM[209 + 2 * j : 210 + 2 * j, :] = row[:, HALF:D]
    SM[216:224, :] = bti
    SM[224:232, 0:IMG] = bto
    SM[224:232, IMG:DS] = jnp.zeros((8, DS - IMG), F32)
    sums = dot(jnp.ones((8, 2 * ROW), BF), mb[both, :])
    SM[232:240, :] = sums[:, 0:HALF]
    SM[240:248, :] = sums[:, HALF:D]
    SB[...] = SM[...].reshape(NY, NZ, 16, DS).astype(BF)

    sr, sl = {}, {}

    def s_reduce(step):
        ref = SB.at[:, Z(5 - step)]
        if step > 1:
            sr[step - 1].wait_recv()
            ref[...] = total(ref[...], SRr[step - 2]).astype(BF)
        sr[step] = put(ref, SRr.at[step - 1], to_z[1])
        if step < 4:
            ref = SB.at[:, Z(step - 4)]
            if step > 1:
                sl[step - 1].wait_recv()
                ref[...] = total(ref[...], SRl[step - 2]).astype(BF)
            sl[step] = put(ref, SRl.at[step - 1], to_z[7])

    s_reduce(1)
    for copy in c_cot:
        copy.wait_send()
    for m in range(NX):
        scot[m] = dot(out_rows(m), lob[0 : 2 * IMG, :]).astype(BF)
    rgrad[x] = scot[x]

    c_xa = []
    for w in (1, 3, 2, 0):
        ra[4, w].wait_recv()
        la[3, w].wait_recv()
        ref = G.at[X(w), z, :, LA]
        ref[...] = total(ref[...], RAr[3, w], RAl[2, w]).astype(BF)
        if w > 0:
            c_xa.append(put(ref, XA.at[w - 1], to_x[w]))
    s_reduce(2)
    b_reduce(1)
    b_reduce(2)
    s_reduce(3)
    arrived(c_xa)
    ref = G.at[x, z, :, LA]
    PY[y, :, LA] = total(ref[...], XA[0], XA[1], XA[2]).astype(BF)
    c_py = [put(PY.at[y, :, LA], PY.at[y, :, LA], to_y[i]) for i in range(1, NY)]
    b_reduce(3)
    s_reduce(4)
    b_reduce(4)
    c_grad = [put(scot.at[X(i)], rgrad.at[x], to_x[i]) for i in range(1, NX)]

    sr[4].wait_recv()
    sl[3].wait_recv()
    ref = SB.at[:, z]
    ref[...] = total(ref[...], SRr[3], SRl[2]).astype(BF)
    c_sx = [put(SB.at[X(i), z], SX.at[i - 1], to_x[i]) for i in range(1, NX)]
    rb[4].wait_recv()
    lb[3].wait_recv()
    PY[y, :, LB] = b_sum(0, [RBr[3], RBl[2]])[...]
    c_py = c_py + [put(PY.at[y, :, LB], PY.at[y, :, LB], to_y[i]) for i in range(1, NY)]
    arrived(c_sx)
    SY[y] = total(SB[x, z], SX[0], SX[1], SX[2]).astype(BF)
    c_sy = [put(SY.at[y], SY.at[y], to_y[i]) for i in range(1, NY)]

    arrived(c_py)
    mean = total(PY[0], PY[1], PY[2], PY[3]) * PER_IMAGE
    H[z, c] = mean.astype(BF)
    hr, hl, hs = {}, {}, {}

    def h_send(step, u, right):
        ref = H.at[Z(1 - step) if right else Z(step - 1), c, 48 * u : 48 * u + 48]
        (hr if right else hl)[step, u] = put(ref, ref, to_z[1] if right else to_z[7])

    def h_share(offset):
        ref = H.at[Z(offset), c]
        hs[offset] = put(ref, ref, sibling)

    for u in range(2):
        h_send(1, u, True)
        h_send(1, u, False)
    h_share(0)

    first_j = used[0]
    used[0] += 3

    def j_copy(i):
        return pltpu.make_async_remote_copy(
            src_ref=H.at[z, c], dst_ref=UJ, send_sem=ssem.at[first_j + i - 1],
            recv_sem=rsem.at[first_j], device_id=to_x[i], device_id_type=MESH,
        )

    @pl.when(x == y)
    def _():
        for i in range(1, NX):
            j_copy(i).start()
        UJ[...] = H[z, c]

    arrived(c_sy)
    SC[c] = total(SY[0], SY[1], SY[2], SY[3]).astype(BF)
    c_sc = put(SC.at[c], SC.at[c], sibling)

    def h_step(step):
        for u in range(2):
            hr[step, u].wait_recv()
            if step < 4:
                h_send(step + 1, u, True)
                hl[step, u].wait_recv()
                if step < 3:
                    h_send(step + 1, u, False)
        h_share(-step)
        if step < 4:
            h_share(step)

    h_step(1)
    c_sc.wait_recv()
    SF[x, z] = (total(SC[0], SC[1]) * PER_IMAGE).astype(BF)
    c_fz = [put(SF.at[x, z], SF.at[x, z], to_z[i]) for i in range(1, NZ)]
    arrived(c_q)
    h_step(2)

    arrived(c_lay)
    arrived(c_grad)

    def of_patch(row, col):
        image = row & 7
        pair, second = image >> 1, image & 1
        return col == PAIR * pair + PATCHES * second + (row >> 3)

    chooser = pick(8 * PATCHES, NX * PAIR, of_patch)
    o_layer[...] = dot(chooser, rlay[...].reshape(NX * PAIR, D)).astype(BF)
    o_gimg[...] = dot(chooser, rgrad[...].reshape(NX * PAIR, D))
    h_step(3)
    arrived(c_fz)
    c_fx = [put(SF.at[x], SF.at[x], to_x[i]) for i in range(1, NX)]

    @pl.when(x != y)
    def _():
        j_copy(1).wait_recv()

    def of_rows(row, col):
        m, i = row >> 4, row & 15
        return (col == 12 * m + i) & (i < 12)

    spread = pick(64, 48, of_rows)
    channels = pick(16, D, lambda row, col: (col == 12 * dp + row) & (row < 12))
    for u, out in enumerate((o_gup, o_gdn)):
        UJP[u, 0:64] = dot(spread, UJ[48 * u : 48 * u + 48, :]).astype(BF)
        UJP[u, 64:80] = channels
        out[...] = UJP[u, pl.ds(pl.multiple_of(16 * x, 16), 16), :][0:12].astype(F32)
    h_step(4)

    arrived([hs[offset] for offset in (0, -1, 1, -2, 2, -3, 3, -4)])
    for u in range(2):
        quarter = H[:, :, 48 * u : 48 * u + 48, :].reshape(D, D)
        right = dot(UJP[u], quarter, 1, 1)
        left = jnp.concatenate([Qx[u].reshape(64, D), right[64:80].astype(BF)], axis=0)
        left = dot(left, quarter)
        for m in range(NX):
            XEo[m, u, :, 0:D] = right[16 * m : 16 * m + 16].astype(BF)
            XEo[m, u, :, D : 2 * D] = left[16 * m : 16 * m + 16].astype(BF)
            XEo[m, u, :, 2 * D : 2 * D + 192] = left[64:80, 192 * m : 192 * m + 192].astype(BF)
            XEo[m, u, :, 2 * D + 192 : 2 * D + 256] = jnp.zeros((16, 64), BF)
    XEi[x] = XEo[x]
    c_xe = [put(XEo.at[X(i)], XEi.at[x], to_x[i]) for i in range(1, NX)]

    arrived(c_fx)
    small = SF[...].reshape(512, DS)
    o_small[0:48, :] = small[208:256].astype(F32)
    o_small[48:64, :] = small[464:480].astype(F32)
    real = lax.broadcasted_iota(jnp.int32, (IMG, DS), 0) < S
    g_in = jnp.where(real, small[0:IMG].astype(F32), 0.0).astype(BF)
    g_out = jnp.where(real, small[IMG : 2 * IMG].astype(F32), 0.0).astype(BF)
    o_lti[...] = 0.5 * ol_ti[...] + 0.5 * dot(g_in, g_in, 1, 1)[0:S, 0:S]
    o_rti[...] = 0.5 * or_ti[...] + 0.5 * dot(g_in, g_in, 0, 0)
    o_lto[...] = 0.5 * ol_to[...] + 0.5 * dot(g_out, g_out, 0, 0)
    o_rto[...] = 0.5 * or_to[...] + 0.5 * dot(g_out, g_out, 1, 1)[0:S, 0:S]
    mine = pick(16, DS, lambda row, col: (col == 6 * dp + row) & (row < 6))
    o_gti[...] = dot(mine, g_in, 1, 1)[0:6, 0:S]
    o_gto[...] = dot(mine, g_out, 1, 1)[0:6, 0:S]
    mine = mine.astype(F32)
    step = dot(mine, pr_ti[...], 1, 1, HIGH)
    step = dot(step, g_in.astype(F32), 1, 1, HIGH)[:, 0:S]
    step = dot(step, pl_ti[...], 1, 1, HIGH)
    o_nti[...] = tin[...] - 0.5 * step[0:6]
    step = dot(mine, pl_to[...], 1, 0, HIGH)
    step = dot(step, g_out.astype(F32), 1, 1, HIGH)[:, 0:S]
    step = dot(step, pr_to[...], 1, 0, HIGH)
    o_nto[...] = tout[...] - 0.5 * step[0:6]

    arrived(c_xe)
    for copy in roots:
        copy.wait()
    for u, (o_stat, old_stat, o_side, old_side, o_new, weight, root, dim) in enumerate((
        (o_rup, old_r_up, o_lup, old_l_up, o_nup, wup, br, 1),
        (o_ldn, old_l_dn, o_rdn, old_r_dn, o_ndn, wdn, dn, 0),
    )):
        for m in range(NX):
            lanes = slice(D * m, D * m + D)
            fresh = XEi[m, u, :, 0:D][0:12].astype(F32)
            o_stat[:, lanes] = 0.5 * old_stat[:, lanes] + 0.5 * fresh
        side = total(*[XEi[m, u, :, 2 * D : 2 * D + 192] for m in range(NX)])
        o_side[...] = 0.5 * old_side[...] + 0.5 * side[0:12]
        step = total(*[XEi[m, u, :, D : 2 * D] for m in range(NX)])
        step = dot(step, root[0:D, :], 1, dim, HIGH)
        o_new[...] = weight[...] - 0.5 * step[0:12]

    for copy in started:
        if not any(copy is other for other in c_img + c_cot):
            copy.wait_send()

    @pl.when(x == y)
    def _():
        for i in range(1, NX):
            j_copy(i).wait_send()


def on_device(
    images, cotangent, image_counts, w_tok_in, w_tok_out, w_up, w_down, norm_params, biases,
    left_tok_in, right_tok_in, left_tok_out, right_tok_out, left_up, right_up, left_down, right_down,
    root_left_tok_in, root_right_tok_in, root_left_tok_out, root_right_tok_out,
    root_left_up, root_right_up, root_left_down, root_right_down, norm_second, bias_second,
):
    patch_rows = 8 * PATCHES

    def by_patch(v):
        return v.transpose(1, 0, 2).reshape(patch_rows, D)

    def by_image(v):
        return v.reshape(PATCHES, 8, D).transpose(1, 0, 2)

    args = (
        image_counts, by_patch(images), by_patch(cotangent), w_tok_in.T, w_tok_out, w_up.T, w_down,
        norm_params, biases[:DS].reshape(DS, 1),
        jnp.pad(biases[DS : DS + S], (0, IMG - S)).reshape(IMG, 1),
        biases[DS + S : DS + S + DC].reshape(NY, NZ, 2, 48).transpose(1, 2, 0, 3).reshape(16, 1, 192),
        biases[DS + S + DC :].reshape(1, D),
        root_right_up.T, root_left_down, root_left_up, root_right_down,
        right_up.T, left_down, left_up, right_down,
        root_left_tok_in, root_right_tok_in, root_left_tok_out, root_right_tok_out,
        left_tok_in, right_tok_in, left_tok_out, right_tok_out,
    )
    outs = [
        ((patch_rows, D), BF), ((patch_rows, D), F32), ((12, D), F32), ((12, D), F32), ((12, D), F32),
        ((12, D), F32), ((12, DC), F32), ((12, DC), F32), ((12, 192), F32), ((12, 192), F32),
        ((64, DS), F32), ((6, S), F32), ((6, S), F32), ((6, S), F32), ((6, S), F32),
        ((S, S), F32), ((DS, DS), F32), ((DS, DS), F32), ((S, S), F32),
    ]

    def vm(dtype, *shape):
        return pltpu.VMEM(shape, dtype)

    scratch = [
        pltpu.SemaphoreType.DMA((256,)), pltpu.SemaphoreType.DMA((256,)), pltpu.SemaphoreType.DMA((2,)),
        vm(F32, 32, DC), vm(BF, 32, D), vm(BF, 16, 256),
        *[vm(BF, NX, PAIR, D) for _ in range(6)],
        vm(BF, NX, 32, D), vm(BF, NY, NZ, 96, D), vm(BF, NY, NZ, 2, 16, 256),
        vm(BF, DS, 256), vm(BF, DS, 256),
        vm(F32, 2, IMG, D), vm(BF, 2, IMG, D), vm(F32, 2, IMG, D), vm(F32, 2, DS, D), vm(BF, 2, DS, D),
        vm(BF, 4 * ROW, D), vm(BF, 4 * ROW, D), vm(F32, 4 * ROW, D), vm(F32, 4 * ROW, D),
        vm(BF, D, D), vm(BF, D, D), vm(BF, 4 * ROW, D), vm(BF, 4 * ROW, D),
        vm(BF, 2, 2 * ROW, D),
        vm(BF, NY, NZ, 96, D),
        vm(BF, 4, NX, 96, HALF), vm(BF, 3, NX, 96, HALF), vm(BF, 3, 96, HALF), vm(BF, 3, NZ, 96, HALF),
        vm(BF, 4, 96, HALF), vm(BF, 3, 96, HALF), vm(BF, NY, 96, D),
        vm(BF, 96, D), vm(BF, 2, 80, D), vm(BF, NZ, 2, 96, D),
        vm(BF, 2, 16, DC), vm(BF, 2, NX, 16, D),
        vm(BF, NX, 2, 16, 1792), vm(BF, NX, 2, 16, 1792),
        vm(F32, 512, DS), vm(BF, NY, NZ, 16, DS), vm(BF, 4, NY, 16, DS), vm(BF, 3, NY, 16, DS),
        vm(BF, 3, 16, DS), vm(BF, NY, 16, DS), vm(BF, 2, 16, DS), vm(BF, NY, NZ, 16, DS),
    ]
    in_vmem = pl.BlockSpec(memory_space=pltpu.VMEM)
    (
        layer, gimg, gup, gdn, nup, ndn, rup, ldn, lup, rdn,
        small, gti, gto, nti, nto, lti, rti, lto, rto,
    ) = pl.pallas_call(
        fused,
        out_shape=[jax.ShapeDtypeStruct(shape, dtype) for shape, dtype in outs],
        in_specs=[pl.BlockSpec(memory_space=pltpu.SMEM)]
        + [pl.BlockSpec(memory_space=pl.ANY) if i in (14, 15) else in_vmem for i in range(1, len(args))],
        out_specs=[in_vmem] * len(outs),
        scratch_shapes=scratch,
        compiler_params=pltpu.CompilerParams(
            collective_id=0, has_side_effects=True, vmem_limit_bytes=64 * 2**20
        ),
        name="fused",
    )(*args)

    norm_grad = small[0:8].reshape(4, D)
    bias_grad = jnp.concatenate([
        small[8], small[16, :S],
        small[48:64, :192].reshape(2, NZ, NY, 48).transpose(2, 1, 0, 3).reshape(DC),
        small[24], small[32],
    ])

    def diagonal_step(current, gradient, second):
        fresh = 0.5 * second + 0.5 * gradient * gradient
        return current - 0.5 * gradient * lax.rsqrt(fresh + 1e-08), fresh

    norm_new, norm_second_new = diagonal_step(norm_params, norm_grad, norm_second)
    bias_new, bias_second_new = diagonal_step(biases, bias_grad, bias_second)
    return (
        by_image(layer), by_image(gimg), gti.T, gto, gup.T, gdn, nti.T, nto, nup.T, ndn,
        lti, rti, lto, rto, lup, rup.T, ldn, rdn,
        norm_grad, norm_second_new, norm_new, bias_grad, bias_second_new, bias_new,
    )


def solution(mesh):
    both, dp, rest = ("dp", "mix"), "dp", P()
    in_specs = (
        P(dp, "mix", None), P(dp, "mix", None), P(dp), P(None, dp), P(dp, None), P(None, both), P(both, None),
        rest, rest, rest, rest, rest, rest,
        P(dp, "mix"), P(None, both), P(both, None), P(dp, "mix"),
        rest, rest, rest, rest, rest, P(None, both), P(both, None), rest, rest, rest,
    )
    out_specs = (
        P(dp, "mix", None), P(dp, "mix", None), P(None, dp), P(dp, None), P(None, both), P(both, None),
        P(None, dp), P(dp, None), P(None, both), P(both, None),
        rest, rest, rest, rest, P(dp, "mix"), P(None, both), P(both, None), P(dp, "mix"),
        rest, rest, rest, rest, rest, rest,
    )
    return jax.shard_map(on_device, mesh=mesh, in_specs=in_specs, out_specs=out_specs, check_vma=False)
```

time: 740 us -> 193 us (0.26)
  waiting for transfers between devices: 248 us -> 0 us
  blocking collectives: 171 us -> 0 us
  Pallas kernels: 0 us -> 165 us
  matrix products: 124 us -> 0 us
  local copies, waits for them, and re-layouts: 102 us -> 22.7 us
  other arithmetic: 54.6 us -> 2.72 us
  starting transfers between devices: 18.7 us -> 0 us
  between operations: 15.4 us -> 1.48 us
    psum x1 -> x0, waiting for transfers between devices: 180 us -> none  [on_device(): lax.psum((tok_in_term, tok_out_term, up_term, down_term, norm_term, bias_...]
    pallas_call x0 -> x1, Pallas kernels: none -> 165 us  [on_device(): pl.pallas_call(fused, out_shape=[jax.ShapeDtypeStruct(shape, dtype) for s...]
    dot_general x28 -> x0, matrix products: 124 us -> none  [the longest x8 38.6 us: renew(): jnp.einsum(pattern, left_operand, right_operand, precision=HIGH, preferre...]
    all_gather x2 -> x0, blocking collectives: 91.7 us -> none  [the longest x1 48.3 us: on_device(): lax.all_gather(w_tok_out.astype(jnp.bfloat16), 'dp', axis=0, tiled=True)]
    psum x1 -> x0, blocking collectives: 79 us -> none  [on_device(): lax.psum((tok_in_term, tok_out_term, up_term, down_term, norm_term, bias_...]
    all_gather x2 -> x0, waiting for transfers between devices: 55.8 us -> none  [the longest x1 55.8 us: on_device(): lax.all_gather(w_down.astype(jnp.bfloat16), ('dp', 'mix'), axis=0, tiled=...]
    unnamed x143 -> x56, local copies, waits for them, and re-layouts: 43.5 us -> 13.5 us
    convert_element_type x9 -> x0, other arithmetic: 20.3 us -> none  [the longest x1 6.22 us: token_forward(): return (pre_tok, gelu_exact(pre_tok).astype(jnp.bfloat16))]
  transfers between devices with their start and end apart: 7 -> 0, of which waited for: 5 -> 0; matrix products, arithmetic and copies ran while one was open for 16% -> 0% of each run, Pallas kernels for 0% -> 0%
where the time goes in v1:
time: 193 us; the launch traced here: 192 us
  Pallas kernels  165 us (85%)
  local copies, waits for them, and re-layouts  22.7 us (12%)
  other arithmetic  2.72 us (1%)
    pallas_call x1, Pallas kernels, on_device(): pl.pallas_call(fused, out_shape=[jax.ShapeDtypeStruct(shape, dtype) for s...  165 us
    unnamed x56, local copies, waits for them, and re-layouts  13.5 us

profile of v1, /device:TPU:1, one launch (start us, length us, event | category | flops | bytes accessed | tf_op | source)
XLA Modules:
  0.0 192.2 jit_solution(8788144339152241112)
XLA Ops:
  1.3 0.7 slice.31
  2.0 0.7 slice.30
  2.7 0.8 slice.33
  4.0 0.8 slice.32
  5.0 0.7 reshape.89.bup
  5.7 0.8 copy.53.btout
  6.5 0.8 reshape.96.btin
  7.3 165.3 %fused.1 = (bf16[392,768]{1,0:T(8,128)(2,1)}, f32[392,768]{1,0:T(8,128)}, f32[12,768]{1,0:T(8,128)}, f32[12,768]{1,0:T(8,128)}, f32[12,768]{1,0:T(8,128)}, /*ind...) custom-call(s32[1]{0:T(128)S(6)} %copy.75.count, ...), custom_call_target="tpu_custom_call" | custom-call | tf_op jit(solution)/shard_map/fused/pallas_call | solution.py:723
  172.7 0.8 slice.36
  173.5 0.8 slice_reduce_fusion
  174.2 0.7 slice.34
  174.9 0.7 slice.37
  176.0 1.4 fusion.3
  177.3 1.4 fusion.1
  178.7 1.9 %copy.76 = bf16[8,49,768]{2,0,1:T(8,128)(2,1)} copy(bf16[8,49,768]{2,0,1:T(8,128)(2,1)} %bitcast.28) | data formatting | bytes 1204224
  180.6 1.0 copy.77
  181.7 0.6 copy.78
  182.3 0.6 copy.79
  182.9 0.6 copy.80
  183.5 0.6 copy.81
  184.1 0.6 copy.82
  184.7 0.6 copy.83
  185.3 0.6 copy.84
  186.0 0.6 copy.85
  186.6 0.7 copy.86
  187.3 0.8 copy.87
  188.1 0.8 copy.88
  188.9 0.7 copy.89
  189.6 0.6 copy.90
  190.2 0.7 copy.91
  190.9 0.7 copy.92
  191.6 0.6 copy.93
  (47 shorter events, 1.1 us)
Async XLA Ops:
  172.6 8.1 %copy-start = (f32[392,768]{1,0:T(8,128)S(1)}, f32[392,768]{1,0:T(8,128)}, u32[]{:S(2)}) copy-start(f32[392,768]{1,0:T(8,128)} %get-tuple-element.44) | copy-start | bytes 3612676
  172.6 9.1 %copy-start.18 = (f32[6,196]{1,0:T(8,128)S(1)}, f32[6,196]{1,0:T(8,128)}, u32[]{:S(2)}) copy-start(f32[6,196]{1,0:T(8,128)} %get-tuple-element.45) | copy-start | bytes 14116
  172.6 9.7 %copy-start.17 = (f32[6,196]{1,0:T(8,128)S(1)}, f32[6,196]{1,0:T(8,128)}, u32[]{:S(2)}) copy-start(f32[6,196]{1,0:T(8,128)} %get-tuple-element.96) | copy-start | bytes 14116
  172.6 10.3 %copy-start.11 = (f32[12,768]{1,0:T(8,128)S(1)}, f32[12,768]{1,0:T(8,128)}, u32[]{:S(2)}) copy-start(f32[12,768]{1,0:T(8,128)} %get-tuple-element.47) | copy-start | bytes 110596
  172.6 10.9 %copy-start.10 = (f32[12,768]{1,0:T(8,128)S(1)}, f32[12,768]{1,0:T(8,128)}, u32[]{:S(2)}) copy-start(f32[12,768]{1,0:T(8,128)} %get-tuple-element.98) | copy-start | bytes 110596
  172.6 11.5 %copy-start.16 = (f32[6,196]{1,0:T(8,128)S(1)}, f32[6,196]{1,0:T(8,128)}, u32[]{:S(2)}) copy-start(f32[6,196]{1,0:T(8,128)} %get-tuple-element.49) | copy-start | bytes 14116
  172.6 12.1 %copy-start.15 = (f32[6,196]{1,0:T(8,128)S(1)}, f32[6,196]{1,0:T(8,128)}, u32[]{:S(2)}) copy-start(f32[6,196]{1,0:T(8,128)} %get-tuple-element.100) | copy-start | bytes 14116
  172.6 12.7 %copy-start.9 = (f32[12,768]{1,0:T(8,128)S(1)}, f32[12,768]{1,0:T(8,128)}, u32[]{:S(2)}) copy-start(f32[12,768]{1,0:T(8,128)} %get-tuple-element.51) | copy-start | bytes 110596
  172.7 13.3 %copy-start.8 = (f32[12,768]{1,0:T(8,128)S(1)}, f32[12,768]{1,0:T(8,128)}, u32[]{:S(2)}) copy-start(f32[12,768]{1,0:T(8,128)} %get-tuple-element.102) | copy-start | bytes 110596
  172.7 13.9 %copy-start.4 = (f32[196,196]{1,0:T(8,128)S(1)}, f32[196,196]{1,0:T(8,128)}, u32[]{:S(2)}) copy-start(f32[196,196]{1,0:T(8,128)} %get-tuple-element.103) | copy-start | bytes 460996
  175.7 11.6 %copy-start.12 = (f32[4,768]{1,0:T(4,128)}, f32[4,768]{1,0:T(4,128)S(1)}, u32[]{:S(2)}) copy-start(f32[4,768]{1,0:T(4,128)S(1)} %reshape.93) | copy-start | bytes 36868
  175.8 11.5 %copy-start.2 = (f32[384,384]{1,0:T(8,128)S(1)}, f32[384,384]{1,0:T(8,128)}, u32[]{:S(2)}) copy-start(f32[384,384]{1,0:T(8,128)} %get-tuple-element.104) | copy-start | bytes 1769476
  176.0 12.1 %copy-start.7 = (f32[4420]{0:T(1024)}, f32[4420]{0:T(1024)S(1)}, u32[]{:S(2)}) copy-start(f32[4420]{0:T(1024)S(1)} %concatenate.3) | copy-start | bytes 53044
  180.6 7.5 %copy-start.1 = (f32[384,384]{1,0:T(8,128)S(1)}, f32[384,384]{1,0:T(8,128)}, u32[]{:S(2)}) copy-start(f32[384,384]{1,0:T(8,128)} %get-tuple-element.105) | copy-start | bytes 1769476
  180.6 8.3 %copy-start.3 = (f32[196,196]{1,0:T(8,128)S(1)}, f32[196,196]{1,0:T(8,128)}, u32[]{:S(2)}) copy-start(f32[196,196]{1,0:T(8,128)} %get-tuple-element.106) | copy-start | bytes 460996
  181.7 7.9 %copy-start.14 = (f32[12,192]{1,0:T(8,128)S(1)}, f32[12,192]{1,0:T(8,128)}, u32[]{:S(2)}) copy-start(f32[12,192]{1,0:T(8,128)} %get-tuple-element.107) | copy-start | bytes 27652
  181.7 8.5 %copy-start.6 = (f32[12,3072]{1,0:T(8,128)S(1)}, f32[12,3072]{1,0:T(8,128)}, u32[]{:S(2)}) copy-start(f32[12,3072]{1,0:T(8,128)} %get-tuple-element.58) | copy-start | bytes 442372
  181.7 9.2 %copy-start.5 = (f32[12,3072]{1,0:T(8,128)S(1)}, f32[12,3072]{1,0:T(8,128)}, u32[]{:S(2)}) copy-start(f32[12,3072]{1,0:T(8,128)} %get-tuple-element.109) | copy-start | bytes 442372
  181.7 9.9 %copy-start.13 = (f32[12,192]{1,0:T(8,128)S(1)}, f32[12,192]{1,0:T(8,128)}, u32[]{:S(2)}) copy-start(f32[12,192]{1,0:T(8,128)} %get-tuple-element.110) | copy-start | bytes 27652

commit v2 on v1

v2 whole, which is shorter than its diff:
```python
import jax
import jax.numpy as jnp
from jax import lax
from jax.experimental import pallas as pl
from jax.experimental.pallas import tpu as pltpu
from jax.sharding import PartitionSpec as P

MESH = pl.DeviceIdType.MESH
BF = jnp.bfloat16
F32 = jnp.float32
HIGH = lax.Precision.HIGHEST

D = 768
DC = 3072
DS = 384
S = 196
NX, NY, NZ = 4, 4, 8
EPS = 1e-06
PER_IMAGE = 1.0 / 512.0
PATCHES = 49
PAIR = 112
IMG = 256
ROW = 208
HALF = D // 2
NB = 4420
NB_ROW = 5120
TILE = 128
P0, P1, P2 = slice(0, 256), slice(256, 512), slice(512, 768)
FAR_FIRST = (4, 5, 3, 6, 2, 7, 1, 0)


def dot(left, right, left_dim=1, right_dim=0, precision=None):
    return lax.dot_general(
        left,
        right,
        (((left_dim,), (right_dim,)), ((), ())),
        preferred_element_type=F32,
        precision=precision,
    )


def pick(rows, cols, rule):
    row = lax.broadcasted_iota(jnp.int32, (rows, cols), 0)
    col = lax.broadcasted_iota(jnp.int32, (rows, cols), 1)
    return jnp.where(rule(row, col), 1.0, 0.0).astype(BF)


def ge(values, bound):
    return (values >= bound).astype(jnp.int32)


def gelu_and_slope(v):
    t = pl.reciprocal(1.0 + 0.23164188 * jnp.abs(v))
    e = jnp.exp(-0.5 * v * v)
    q = 0.5 * t * (
        0.254829592 + t * (-0.284496736 + t * (1.421413741 + t * (-1.453152027 + t * 1.061405429)))
    ) * e
    cdf = jnp.where(v >= 0, 1.0 - q, q)
    return v * cdf, cdf + v * e * 0.3989422804014327


def normalise(v):
    mean = jnp.mean(v, axis=-1, keepdims=True)
    centre = v - mean
    r = lax.rsqrt(jnp.mean(centre * centre, axis=-1, keepdims=True) + EPS)
    return centre * r, r


def normalise_back(xhat, r, dh, gain):
    dxh = dh * gain
    m1 = jnp.mean(dxh, axis=-1, keepdims=True)
    m2 = jnp.mean(dxh * xhat, axis=-1, keepdims=True)
    dv = r * (dxh - m1 - xhat * m2)
    return dv, jnp.sum(dh * xhat, axis=0, keepdims=True), jnp.sum(dh, axis=0, keepdims=True)


def fused(
    count, img, cot, tin, tout, wup, wdn, norm, bias,
    q_up, p_dn, p_up, q_dn, old_r_up, old_l_dn, old_l_up, old_r_dn,
    pl_ti, pr_ti, pl_to, pr_to, ol_ti, or_ti, ol_to, or_to,
    rlay, rgrad, o_gup, o_gdn, o_nup, o_ndn, o_rup, o_ldn, o_lup, o_rdn,
    o_norm, o_bias, o_gti, o_gto, o_nti, o_nto, o_lti, o_rti, o_lto, o_rto,
    ssem, rsem, lsem, stage, wst, tst, simg, scot, rimg, rcot,
    xw, W, tk, tokin, tokout, bti, bto, bup, ximg, normed, mid, slope, act, n2, mb, br, dn,
    upc, dnc, actb, dpb, xbi, G, RAr, RAl, XA, YA, XB, YB, YC, XD, PZ, RZ,
    HQ, UJQ, UJP, qst, Qx, XEo, XEi, SM, SB, SX, SZ, SY, SC, SF,
):
    dp = lax.axis_index("dp")
    x = lax.axis_index("mix")
    c = lax.rem(dp, 2)
    y = dp // (2 * NZ)
    z = lax.rem(dp // 2, NZ)

    def X(i):
        return lax.rem(x + i + NX, NX)

    def Y(i):
        return lax.rem(y + i + NY, NY)

    def Z(i):
        return lax.rem(z + i + NZ, NZ)

    def dev(xx, yy, zz, cc):
        return ((yy * NZ + zz) * 2 + cc, xx)

    to_x = [None] + [dev(X(i), y, z, c) for i in range(1, NX)]
    to_y = [None] + [dev(x, Y(i), z, c) for i in range(1, NY)]
    to_z = [None] + [dev(x, y, Z(i), c) for i in range(1, NZ)]
    sibling = dev(x, y, z, 1 - c)
    started = []
    used = [0]

    def put(src, dst, device):
        k = used[0]
        used[0] += 1
        copy = pltpu.make_async_remote_copy(
            src_ref=src, dst_ref=dst, send_sem=ssem.at[k], recv_sem=rsem.at[k],
            device_id=device, device_id_type=MESH,
        )
        copy.start()
        started.append(copy)
        return copy

    def arrived(copies):
        for copy in copies:
            copy.wait_recv()

    def settle(copies):
        for copy in copies:
            copy.wait_send()
        started[:] = [item for item in started if not any(item is copy for copy in copies)]

    def total(*parts):
        value = parts[0].astype(F32)
        for part in parts[1:]:
            value = value + part.astype(F32)
        return value

    barrier = pltpu.get_barrier_semaphore()
    peers = to_x[1:] + to_y[1:] + to_z[1:] + [sibling]
    for peer in peers:
        pl.semaphore_signal(barrier, inc=1, device_id=peer, device_id_type=MESH)

    stage[:, 0 : 2 * D] = jnp.zeros((32, 2 * D), F32)
    stage[0:12, 0:D] = wup[...]
    stage[16:28, 0:D] = wdn[...]
    stage[0:6, D : D + S] = tin[...]
    stage[8:14, D : D + S] = tout[...]
    wst[...] = stage[:, 0:D].astype(BF)
    tst[...] = stage[0:16, D : D + 256].astype(BF)
    xw[x] = wst[...]
    tk[y, z, c] = tst[...]

    pl.semaphore_wait(barrier, len(peers))
    c_xw = [put(wst, xw.at[x], to_x[i]) for i in range(1, NX)]
    c_ty = [put(tk.at[y, z, c], tk.at[y, z, c], to_y[i]) for i in range(1, NY)]

    def of_pairs(row, col):
        m = ge(row, PAIR) + ge(row, 2 * PAIR) + ge(row, 3 * PAIR)
        i = row - PAIR * m
        second = ge(i, PATCHES)
        return (col == (i - PATCHES * second) * 8 + 2 * m + second) & (i < 2 * PATCHES)

    chooser = pick(NX * PAIR, 8 * PATCHES, of_pairs)
    simg[...] = dot(chooser, img[...]).astype(BF).reshape(NX, PAIR, D)
    c_img = [put(simg.at[X(i)], rimg.at[x], to_x[i]) for i in range(1, NX)]

    arrived(c_xw)

    def of_shards(row, col):
        m, j = col >> 5, col & 31
        up = (j < 12) & (row == 12 * m + j)
        down = (j >= 16) & (j < 28) & (row == 32 + 12 * m + j)
        return up | down

    upc[0:96, :] = dot(pick(96, 128, of_shards), xw[...].reshape(128, D)).astype(BF)
    W[y, z, :, 0:512] = upc[0:96, 0:512]

    def rows_of(q):
        return pl.ds(pl.multiple_of(48 * (q // 2), 16), 48)

    def lanes_of(q, part):
        return pl.ds(pl.multiple_of(256 * part + TILE * lax.rem(q, 2), TILE), TILE)

    a_right, a_left, b_right, b_left, b_y = {}, {}, {}, {}, {}

    def a_send(step, d, right):
        if right:
            ref = W.at[Y(-d), Z(1 - step), :, P0]
            a_right[step, d] = put(ref, ref, to_z[1])
        else:
            ref = W.at[Y(-d), Z(step - 1), :, P0]
            a_left[step, d] = put(ref, ref, to_z[7])

    def b_send(step, right):
        if right:
            ref = W.at[y, Z(1 - step), :, P1]
            b_right[step] = put(ref, ref, to_z[1])
        else:
            ref = W.at[y, Z(step - 1), :, P1]
            b_left[step] = put(ref, ref, to_z[7])

    def b_spread(offset):
        ref = W.at[y, Z(offset), :, P1]
        b_y[offset] = [put(ref, ref, to_y[i]) for i in range(1, NY)]

    def c_ref(yy, zz):
        return W.at[yy, zz, rows_of(x), lanes_of(x, 2)]

    def c_spread(d):
        ref = c_ref(Y(-d), slice(None))
        return [put(ref, ref, to_x[i]) for i in range(1, NX)]

    W[y, z, rows_of(x), lanes_of(x, 2)] = upc[rows_of(x), lanes_of(x, 2)]
    own_a = W.at[y, z, :, P0]
    b_send(1, True)
    b_send(1, False)
    c_ay = [None] + [put(own_a, own_a, to_y[i]) for i in range(1, NY)]
    c_cz = [put(c_ref(y, z), c_ref(y, z), to_z[i]) for i in range(1, NZ)]
    arrived(c_ty)
    c_tz = [put(tk.at[:, z, c], tk.at[:, z, c], to_z[i]) for i in range(1, NZ)]
    a_send(1, 0, True)
    a_send(1, 0, False)
    b_spread(0)
    for d in (1, 3, 2):
        c_ay[d].wait_recv()
        a_send(1, d, True)
        a_send(1, d, False)

    scot[...] = dot(chooser, cot[...]).astype(BF).reshape(NX, PAIR, D)
    c_cot = [put(scot.at[X(i)], rcot.at[x], to_x[i]) for i in range(1, NX)]
    rimg[x] = simg[x]
    rcot[x] = scot[x]
    stage[0:12, :] = q_up[...]
    stage[12:16, :] = jnp.zeros((4, DC), F32)
    stage[16:28, :] = p_dn[...]
    stage[28:32, :] = jnp.zeros((4, DC), F32)
    qst[0] = stage[0:16, :].astype(BF)
    qst[1] = stage[16:32, :].astype(BF)
    diagonal = pick(TILE, TILE, lambda row, col: row == col).astype(F32)

    def column(first):
        spread = jnp.broadcast_to(bias[:, first : first + TILE], (TILE, TILE))
        return jnp.sum(spread * diagonal, axis=1, keepdims=True)

    for j in range(3):
        bti[TILE * j : TILE * j + TILE, :] = column(TILE * j)
    for j in range(2):
        bto[TILE * j : TILE * j + TILE, :] = column(DS + TILE * j)
    for zz in range(NZ):
        for cc in range(2):
            first = [DS + S + 48 * ((yy * NZ + zz) * 2 + cc) for yy in range(NY)]
            bup[2 * zz + cc] = jnp.concatenate([bias[:, f : f + 48] for f in first], axis=1)
    bias_down = bias[:, DS + S + DC : NB]

    arrived(c_cz)
    c_cy = [None] + [put(c_ref(y, slice(None)), c_ref(y, slice(None)), to_y[i]) for i in range(1, NY)]
    c_cx = c_spread(0)

    def gather_step(step):
        b_right[step].wait_recv()
        if step < 4:
            b_send(step + 1, True)
        b_spread(-step)
        if step < 4:
            b_left[step].wait_recv()
            if step < 3:
                b_send(step + 1, False)
            b_spread(step)
        for d in (0, 1, 3, 2):
            a_right[step, d].wait_recv()
            if step < 4:
                a_send(step + 1, d, True)
                a_left[step, d].wait_recv()
                if step < 3:
                    a_send(step + 1, d, False)

    arrived(c_tz)
    c_tc = put(tk.at[:, :, c], tk.at[:, :, c], sibling)
    gather_step(1)
    for d in (1, 3, 2):
        c_cy[d].wait_recv()
        c_cx = c_cx + c_spread(d)
    c_tc.wait_recv()

    def of_group(row, col):
        group, i = col >> 4, col & 15
        first = (i < 6) & (row == 6 * group + i)
        second = (i >= 8) & (i < 14) & (row == 40 + 6 * group + i)
        return first | second

    chooser = pick(96, 128, of_group)
    for g in range(8):
        part = tk[g // 2, 4 * (g % 2) : 4 * (g % 2) + 4].reshape(128, 256)
        part = dot(chooser, part).astype(BF)
        tokin[48 * g : 48 * g + 48, :] = part[0:48]
        tokout[48 * g : 48 * g + 48, :] = part[48:96]

    arrived(c_img)
    arrived(c_cot)
    keep = [jnp.where(2 * x + b < count[0], 1.0, 0.0).astype(F32) for b in range(2)]
    own = c * (2 * ROW)

    def own_rows(b):
        return pl.ds(pl.multiple_of(own + b * ROW, 16), ROW)

    both = pl.ds(pl.multiple_of(own, 16), 2 * ROW)

    def of_images(row, col):
        b = ge(row, IMG)
        i = row - IMG * b
        part = ge(i, 49) + ge(i, 98) + ge(i, 147)
        return (col == 63 * part + 49 * b + i) & (i < S)

    chooser = pick(2 * IMG, NX * PAIR, of_images)
    ximg[...] = dot(chooser, rimg[...].reshape(NX * PAIR, D)).reshape(2, IMG, D)
    back = dot(chooser, rcot[...].reshape(NX * PAIR, D))
    for b in range(2):
        mb[own_rows(b), :] = (back[b * IMG : b * IMG + ROW] * keep[b]).astype(BF)
        xhat, _ = normalise(ximg[b])
        normed[b] = (xhat * norm[0:1, :] + norm[1:2, :]).astype(BF)
    c_mb = put(mb.at[both], mb.at[both], sibling)
    gather_step(2)

    @pl.loop(0, 2)
    def _(b):
        pre = dot(tokin[...], normed[b]) + bti[...]
        value, grad = gelu_and_slope(pre)
        slope[b] = grad
        act[b] = value.astype(BF)
        mixed = dot(tokout[...], act[b], 0, 0) + bto[...]
        middle = ximg[b] + mixed.astype(BF).astype(F32)
        mid[b] = middle
        xhat, _ = normalise(middle[0:ROW])
        n2[own_rows(b), :] = (xhat * norm[2:3, :] + norm[3:4, :]).astype(BF)

    c_n2 = put(n2.at[both], n2.at[both], sibling)
    gather_step(3)
    gather_step(4)
    for offset in (0, -1, 1, -2, 2, -3, 3, -4):
        arrived(b_y[offset])
    arrived(c_cx)
    c_mb.wait_recv()
    c_n2.wait_recv()

    br[...] = jnp.zeros_like(br)
    dn[...] = jnp.zeros_like(dn)
    for half in range(2):
        offsets = FAR_FIRST[4 * half : 4 * half + 4]
        for j, k in enumerate(offsets):
            upc[192 * j : 192 * j + 192, :] = W[:, Z(k), 0:48, :].reshape(192, D)
            dnc[192 * j : 192 * j + 192, :] = W[:, Z(k), 48:96, :].reshape(192, D)
        row = jnp.concatenate([bup[2 * Z(k) + c] for k in offsets], axis=1)
        lanes = slice(half * D, half * D + D)

        @pl.loop(0, 4)
        def _(r, row=row, lanes=lanes):
            rows = pl.ds(pl.multiple_of(r * ROW, 16), ROW)
            pre = dot(n2[rows, :], upc[...], 1, 1) + row
            value, grad = gelu_and_slope(pre)
            low = value.astype(BF)
            actb[rows, lanes] = low
            br[rows, :] += dot(low, dnc[...])
            low = (grad * dot(mb[rows, :], dnc[...], 1, 1)).astype(BF)
            dpb[rows, lanes] = low
            dn[rows, :] += dot(low, upc[...])

    other = pl.ds(pl.multiple_of((1 - c) * (2 * ROW), 16), 2 * ROW)
    upc[0 : 2 * ROW, :] = dn[other, :].astype(BF)
    c_dn = put(upc.at[0 : 2 * ROW], xbi.at[1], sibling)
    dnc[0 : 2 * ROW, :] = br[other, :].astype(BF)
    c_br = put(dnc.at[0 : 2 * ROW], xbi.at[0], sibling)

    ra, la, xb, yb, yc, xd, rz = {}, {}, {}, {}, {}, {}, {}

    def gradients(pair):
        lanes = slice(2 * 192 * pair, 2 * 192 * pair + 384)
        offsets = FAR_FIRST[2 * pair : 2 * pair + 2]
        for u, (left, right) in enumerate(((dpb, n2), (actb, mb))):
            grad = dot(left[:, lanes], right[...], 0, 0).astype(BF)
            for j, k in enumerate(offsets):
                part = grad[192 * j : 192 * j + 192].reshape(4, 48, D)
                G[:, Z(k), 48 * u : 48 * u + 48, :] = part
        for k in offsets:
            for i in range(1, NX):
                xb[k, i] = put(G.at[X(i), Z(k), :, P1], XB.at[i - 1, Z(k)], to_x[i])
                ref = G.at[:, Z(k), rows_of(Y(i)), lanes_of(Y(i), 2)]
                yb[k, i] = put(ref, YB.at[i - 1, Z(k)], to_y[i])

    def a_reduce(step):
        for w in range(NX):
            ref = G.at[X(w), Z(5 - step), :, P0]
            if step > 1:
                ra[step - 1, w].wait_recv()
                ref[...] = total(ref[...], RAr[step - 2, w]).astype(BF)
            ra[step, w] = put(ref, RAr.at[step - 1, w], to_z[1])
            if step < 4:
                ref = G.at[X(w), Z(step - 4), :, P0]
                if step > 1:
                    la[step - 1, w].wait_recv()
                    ref[...] = total(ref[...], RAl[step - 2, w]).astype(BF)
                la[step, w] = put(ref, RAl.at[step - 1, w], to_z[7])

    def second(k):
        arrived([xb[k, i] for i in range(1, NX)])
        ref = G.at[x, Z(k), :, P1]
        ref[...] = total(ref[...], *[XB[i, Z(k)] for i in range(NX - 1)]).astype(BF)
        for i in range(1, NY):
            ref = G.at[x, Z(k), rows_of(Y(i)), lanes_of(Y(i), 1)]
            yc[k, i] = put(ref, YC.at[i - 1, Z(k)], to_y[i])
        arrived([yb[k, i] for i in range(1, NY)])
        ref = G.at[:, Z(k), rows_of(y), lanes_of(y, 2)]
        ref[...] = total(ref[...], *[YB[i, Z(k)] for i in range(NY - 1)]).astype(BF)
        for i in range(1, NX):
            ref = G.at[X(i), Z(k), rows_of(y), lanes_of(y, 2)]
            xd[k, i] = put(ref, XD.at[i - 1, Z(k)], to_x[i])

    def third(k):
        arrived([yc[k, i] for i in range(1, NY)])
        value = G[x, Z(k), rows_of(y), lanes_of(y, 1)]
        PZ[Z(k), :, 0:TILE] = total(value, *[YC[i, Z(k)] for i in range(NY - 1)]).astype(BF)
        arrived([xd[k, i] for i in range(1, NX)])
        value = G[x, Z(k), rows_of(y), lanes_of(y, 2)]
        PZ[Z(k), :, TILE : 2 * TILE] = total(value, *[XD[i, Z(k)] for i in range(NX - 1)]).astype(BF)
        if k > 0:
            rz[k] = put(PZ.at[Z(k)], RZ.at[k - 1], to_z[k])

    gradients(0)
    a_reduce(1)
    gradients(1)
    gradients(2)
    a_reduce(2)
    gradients(3)

    c_dn.wait_recv()
    c_br.wait_recv()
    ones = jnp.ones((8, 4 * ROW), BF)
    up_sums = dot(ones, dpb[...])[0:1]
    down_sums = dot(ones[:, 0 : 2 * ROW], mb[both, :])
    lob, dmx = actb, dpb
    lob[0 : 2 * IMG, 0:D] = jnp.zeros((2 * IMG, D), BF)
    dmx[0 : 2 * IMG, 0:D] = jnp.zeros((2 * IMG, D), BF)
    gain_two = jnp.zeros((1, D), F32)
    shift_two = jnp.zeros((1, D), F32)
    for b in range(2):
        here = slice(b * ROW, b * ROW + ROW)
        branch = br[own_rows(b), :] + xbi[0, here, :].astype(F32) + bias_down
        lob[b * IMG : b * IMG + ROW, 0:D] = (keep[b] * (mid[b, 0:ROW] + branch)).astype(BF)
        dh = dn[own_rows(b), :] + xbi[1, here, :].astype(F32)
        xhat, r = normalise(mid[b, 0:ROW])
        dv, gain, shift = normalise_back(xhat, r, dh, norm[2:3, :])
        gain_two = gain_two + gain
        shift_two = shift_two + shift
        back = mb[own_rows(b), :].astype(F32) + dv
        mid[b, 0:ROW] = back
        dmx[b * IMG : b * IMG + ROW, 0:D] = back.astype(BF)

    def of_out(row, col):
        m = ge(row, PAIR) + ge(row, 2 * PAIR) + ge(row, 3 * PAIR)
        i = row - PAIR * m
        second_one = ge(i, PATCHES)
        place = (IMG - PATCHES) * second_one + PATCHES * m + i
        return (col == place) & (i < 2 * PATCHES)

    out_chooser = pick(NX * PAIR, 2 * IMG, of_out)

    def to_patches(buffer, sent):
        settle(sent)
        buffer[...] = dot(out_chooser, lob[0 : 2 * IMG, 0:D]).astype(BF).reshape(NX, PAIR, D)

    second(4)
    second(5)
    a_reduce(3)
    to_patches(simg, c_img)
    own_out = [pltpu.make_async_copy(simg.at[x], rlay.at[x], lsem.at[2])]
    own_out[0].start()
    c_lay = [put(simg.at[X(i)], rlay.at[x], to_x[i]) for i in range(1, NX)]
    second(3)
    second(6)

    roots = [
        pltpu.make_async_copy(p_up, br.at[0:D], lsem.at[0]),
        pltpu.make_async_copy(q_dn, dn.at[0:D], lsem.at[1]),
    ]
    for copy in roots:
        copy.start()
    gti = jnp.zeros((IMG, DS), F32)
    gto = jnp.zeros((IMG, DS), F32)
    sum_ti = jnp.zeros((8, DS), F32)
    sum_to = jnp.zeros((8, IMG), F32)
    gain_one = jnp.zeros((1, D), F32)
    shift_one = jnp.zeros((1, D), F32)
    ones = jnp.ones((8, D), BF)
    for b in range(2):
        dmixed = dmx[b * IMG : b * IMG + IMG, 0:D]
        dpre = (slope[b] * dot(tokout[...], dmixed)).astype(BF)
        gti = gti + dot(normed[b], dpre, 1, 1)
        gto = gto + dot(dmixed, act[b], 1, 1)
        sum_ti = sum_ti + dot(ones, dpre, 1, 1)
        sum_to = sum_to + dot(ones, dmixed, 1, 1)
        dnormed = dot(tokin[...], dpre, 0, 0).astype(BF).astype(F32)
        xhat, r = normalise(ximg[b, 0:ROW])
        dv, gain, shift = normalise_back(xhat, r, dnormed[0:ROW], norm[0:1, :])
        gain_one = gain_one + gain
        shift_one = shift_one + shift
        lob[b * IMG : b * IMG + ROW, 0:D] = (mid[b, 0:ROW] + dv).astype(BF)
        if b == 0:
            a_reduce(4)
            second(2)
            second(7)
            third(4)
            third(5)
        else:
            second(1)
            second(0)
            third(3)
            third(6)

    SM[0:IMG, :] = gti
    SM[IMG : IMG + ROW, :] = gto[0:ROW]
    SM[IMG + ROW :, :] = jnp.zeros((IMG - ROW, DS), F32)
    for j, row in enumerate((gain_one, shift_one, gain_two, shift_two)):
        SM[208 + 2 * j : 209 + 2 * j, :] = row[:, 0:HALF]
        SM[209 + 2 * j : 210 + 2 * j, :] = row[:, HALF:D]
    SM[216:224, :] = sum_ti
    SM[224:232, 0:IMG] = sum_to
    SM[224:232, IMG:DS] = jnp.zeros((8, DS - IMG), F32)
    SM[232:240, :] = down_sums[:, 0:HALF]
    SM[240:248, :] = down_sums[:, HALF:D]
    for j, k in enumerate(FAR_FIRST):
        SM[pl.ds(464 + 8 * c + Z(k), 1), 0:192] = up_sums[:, 192 * j : 192 * j + 192]
    SB[...] = SM[...].reshape(NY, NZ, 16, DS).astype(BF)
    c_sx = [put(SB.at[X(i)], SX.at[i - 1], to_x[i]) for i in range(1, NX)]

    c_xa = []
    for w in (1, 3, 2, 0):
        ra[4, w].wait_recv()
        la[3, w].wait_recv()
        ref = G.at[X(w), z, :, P0]
        ref[...] = total(ref[...], RAr[3, w], RAl[2, w]).astype(BF)
        if w > 0:
            c_xa.append(put(ref, XA.at[w - 1], to_x[w]))
    for k in (2, 7, 1, 0):
        third(k)
    arrived(c_xa)
    ref = G.at[x, z, :, P0]
    ref[...] = total(ref[...], XA[0], XA[1], XA[2]).astype(BF)
    c_ya = [
        put(G.at[x, z, rows_of(Y(i)), lanes_of(Y(i), 0)], YA.at[i - 1], to_y[i])
        for i in range(1, NY)
    ]
    arrived(c_sx)
    SB[x] = total(SB[x], SX[0], SX[1], SX[2]).astype(BF)
    c_sz = [put(SB.at[x, Z(i)], SZ.at[i - 1], to_z[i]) for i in range(1, NZ)]

    arrived(rz.values())
    mean = total(PZ[z], *[RZ[i] for i in range(NZ - 1)]) * PER_IMAGE
    HQ[c, y, z, :, TILE:] = mean.astype(BF)
    arrived(c_ya)
    mean = total(G[x, z, rows_of(y), lanes_of(y, 0)], YA[0], YA[1], YA[2]) * PER_IMAGE
    HQ[c, y, z, :, 0:TILE] = mean.astype(BF)
    hz, hy, hs = {}, {}, {}
    for i in (4, 3, 5, 2, 6, 1, 7):
        hz[i] = put(HQ.at[c, y, z], HQ.at[c, y, z], to_z[i])

    def h_spread(offset):
        ref = HQ.at[c, y, Z(offset)]
        hy[offset] = [put(ref, ref, to_y[i]) for i in range(1, NY)]

    def h_share(offset):
        arrived(hy[offset])
        ref = HQ.at[c, :, Z(offset)]
        hs[offset] = put(ref, ref, sibling)

    h_spread(0)
    to_patches(scot, c_cot)
    own_out.append(pltpu.make_async_copy(scot.at[x], rgrad.at[x], lsem.at[3]))
    own_out[1].start()
    c_grad = [put(scot.at[X(i)], rgrad.at[x], to_x[i]) for i in range(1, NX)]
    arrived(c_sz)
    SY[y] = total(SB[x, z], *[SZ[i] for i in range(NZ - 1)]).astype(BF)
    c_sy = [put(SY.at[y], SY.at[y], to_y[i]) for i in range(1, NY)]
    for i in (1, 7, 2, 6):
        hz[i].wait_recv()
        h_spread(-i)
    h_share(0)

    first_j = used[0]
    used[0] += 3

    def j_copy(i):
        return pltpu.make_async_remote_copy(
            src_ref=HQ.at[c, :, z], dst_ref=UJQ, send_sem=ssem.at[first_j + i - 1],
            recv_sem=rsem.at[first_j], device_id=to_x[i], device_id_type=MESH,
        )

    @pl.when(x == y)
    def _():
        for i in range(1, NX):
            j_copy(i).start()
        UJQ[...] = HQ[c, :, z]

    arrived(c_sy)
    SC[c] = total(SY[0], SY[1], SY[2], SY[3]).astype(BF)
    c_sc = put(SC.at[c], SC.at[c], sibling)
    for i in (3, 5, 4):
        hz[i].wait_recv()
        h_spread(-i)
    c_sc.wait_recv()
    SF[x, z] = (total(SC[0], SC[1]) * PER_IMAGE).astype(BF)
    c_fz = [put(SF.at[x, z], SF.at[x, z], to_z[i]) for i in range(1, NZ)]
    for i in (1, 7, 2, 6):
        h_share(-i)
    Qx[:, x] = qst[:, :, pl.ds(pl.multiple_of(x * D, D), D)]
    c_q = [
        put(qst.at[:, :, pl.ds(pl.multiple_of(X(i) * D, D), D)], Qx.at[:, x], to_x[i])
        for i in range(1, NX)
    ]

    @pl.when(x != y)
    def _():
        j_copy(1).wait_recv()

    def of_rows(row, col):
        m, i = row >> 4, row & 15
        return (col == 12 * m + i) & (i < 12)

    spread = pick(64, 48, of_rows)
    channels = pick(16, D, lambda row, col: (col == 12 * dp + row) & (row < 12))

    def unfold(dst, read, u):
        for t in range(2):
            value = read(2 * u + t)
            for part in range(3):
                lanes = slice(256 * part + TILE * t, 256 * part + TILE * t + TILE)
                dst[:, lanes] = value[..., TILE * part : TILE * part + TILE].reshape(-1, TILE)

    settle([c_dn, c_mb, c_n2])
    for u, out in enumerate((o_gup, o_gdn)):
        unfold(upc.at[0:48], lambda q: UJQ[q], u)
        UJP[u, 0:64] = dot(spread, upc[0:48, :]).astype(BF)
        UJP[u, 64:80] = channels
        out[...] = UJP[u, pl.ds(pl.multiple_of(16 * x, 16), 16), :][0:12].astype(F32)
    arrived(c_fz)
    c_fx = [put(SF.at[x], SF.at[x], to_x[i]) for i in range(1, NX)]
    for i in (3, 5, 4):
        h_share(-i)

    arrived([hs[offset] for offset in (0, -1, -7, -2, -6, -3, -5, -4)])
    arrived(c_q)
    for u in range(2):
        store = (n2, mb)[u]
        for zz in range(NZ):
            for cc in range(2):
                first = (2 * zz + cc) * 48
                unfold(store.at[first : first + 48], lambda q: HQ[cc, q, zz], u)
        quarter = store[0:D, :]
        right = dot(UJP[u], quarter, 1, 1)
        left = jnp.concatenate([Qx[u].reshape(64, D), right[64:80].astype(BF)], axis=0)
        left = dot(left, quarter)
        for m in range(NX):
            XEo[m, u, :, 0:D] = right[16 * m : 16 * m + 16].astype(BF)
            XEo[m, u, :, D : 2 * D] = left[16 * m : 16 * m + 16].astype(BF)
            XEo[m, u, :, 2 * D : 2 * D + 192] = left[64:80, 192 * m : 192 * m + 192].astype(BF)
            XEo[m, u, :, 2 * D + 192 : 2 * D + 256] = jnp.zeros((16, 64), BF)
    XEi[x] = XEo[x]
    c_xe = [put(XEo.at[X(i)], XEi.at[x], to_x[i]) for i in range(1, NX)]

    arrived(c_fx)
    small = SF[...].reshape(512, DS)
    o_norm[...] = small[208:216].astype(F32)
    vector = small[208:256].astype(F32)
    ups = small[464:480].astype(F32)
    pieces = [vector[8:9], vector[16:17, 0:S]]
    for yy in range(NY):
        for zz in range(NZ):
            for cc in range(2):
                pieces.append(ups[8 * cc + zz : 8 * cc + zz + 1, 48 * yy : 48 * yy + 48])
    pieces += [vector[24:25], vector[32:33], jnp.zeros((1, NB_ROW - NB), F32)]
    o_bias[...] = jnp.concatenate(pieces, axis=1)
    real = lax.broadcasted_iota(jnp.int32, (IMG, DS), 0) < S
    g_in = jnp.where(real, small[0:IMG].astype(F32), 0.0).astype(BF)
    g_out = jnp.where(real, small[IMG : 2 * IMG].astype(F32), 0.0).astype(BF)
    o_lti[...] = 0.5 * ol_ti[...] + 0.5 * dot(g_in, g_in, 1, 1)[0:S, 0:S]
    o_rti[...] = 0.5 * or_ti[...] + 0.5 * dot(g_in, g_in, 0, 0)
    o_lto[...] = 0.5 * ol_to[...] + 0.5 * dot(g_out, g_out, 0, 0)
    o_rto[...] = 0.5 * or_to[...] + 0.5 * dot(g_out, g_out, 1, 1)[0:S, 0:S]
    mine = pick(16, DS, lambda row, col: (col == 6 * dp + row) & (row < 6))
    o_gti[...] = dot(mine, g_in, 1, 1)[0:6, 0:S]
    o_gto[...] = dot(mine, g_out, 1, 1)[0:6, 0:S]
    mine = mine.astype(F32)
    step = dot(mine, pr_ti[...], 1, 1, HIGH)
    step = dot(step, g_in.astype(F32), 1, 1, HIGH)[:, 0:S]
    step = dot(step, pl_ti[...], 1, 1, HIGH)
    o_nti[...] = tin[...] - 0.5 * step[0:6]
    step = dot(mine, pl_to[...], 1, 0, HIGH)
    step = dot(step, g_out.astype(F32), 1, 1, HIGH)[:, 0:S]
    step = dot(step, pr_to[...], 1, 0, HIGH)
    o_nto[...] = tout[...] - 0.5 * step[0:6]

    arrived(c_xe)
    for copy in roots:
        copy.wait()
    for u, (o_stat, old_stat, o_side, old_side, o_new, weight, root, dim) in enumerate((
        (o_rup, old_r_up, o_lup, old_l_up, o_nup, wup, br, 1),
        (o_ldn, old_l_dn, o_rdn, old_r_dn, o_ndn, wdn, dn, 0),
    )):
        for m in range(NX):
            lanes = slice(D * m, D * m + D)
            fresh = XEi[m, u, :, 0:D][0:12].astype(F32)
            o_stat[:, lanes] = 0.5 * old_stat[:, lanes] + 0.5 * fresh
        side = total(*[XEi[m, u, :, 2 * D : 2 * D + 192] for m in range(NX)])
        o_side[...] = 0.5 * old_side[...] + 0.5 * side[0:12]
        step = total(*[XEi[m, u, :, D : 2 * D] for m in range(NX)])
        step = dot(step, root[0:D, :], 1, dim, HIGH)
        o_new[...] = weight[...] - 0.5 * step[0:12]

    arrived(c_lay)
    arrived(c_grad)
    for copy in own_out:
        copy.wait()
    settle(list(started))

    @pl.when(x == y)
    def _():
        for i in range(1, NX):
            j_copy(i).wait_send()


def finish(
    rlay, rgrad, grads, norm, second, *refs
):
    handed = (len(refs) - 5) // 2
    sources, outs = refs[:handed], refs[handed:]
    o_layer, o_gimg, o_grad, o_second, o_norm = outs[handed:]
    for src, dst in zip(sources, outs):
        dst[...] = src[...]

    def of_patch(row, col):
        image = row & 7
        pair, second_one = image >> 1, image & 1
        return col == PAIR * pair + PATCHES * second_one + (row >> 3)

    chooser = pick(8 * PATCHES, NX * PAIR, of_patch)
    o_layer[...] = dot(chooser, rlay[...].reshape(NX * PAIR, D)).astype(BF)
    o_gimg[...] = dot(chooser, rgrad[...].reshape(NX * PAIR, D))
    for j in range(4):
        row = slice(j, j + 1)
        grad = jnp.concatenate([grads[2 * j : 2 * j + 1, :], grads[2 * j + 1 : 2 * j + 2, :]], axis=1)
        fresh = 0.5 * second[row, :] + 0.5 * grad * grad
        o_grad[row, :] = grad
        o_second[row, :] = fresh
        o_norm[row, :] = norm[row, :] - 0.5 * grad * lax.rsqrt(fresh + 1e-08)


def on_device(
    images, cotangent, image_counts, w_tok_in, w_tok_out, w_up, w_down, norm_params, biases,
    left_tok_in, right_tok_in, left_tok_out, right_tok_out, left_up, right_up, left_down, right_down,
    root_left_tok_in, root_right_tok_in, root_left_tok_out, root_right_tok_out,
    root_left_up, root_right_up, root_left_down, root_right_down, norm_second, bias_second,
):
    patch_rows = 8 * PATCHES

    def by_patch(v):
        return v.transpose(1, 0, 2).reshape(patch_rows, D)

    def by_image(v):
        return v.reshape(PATCHES, 8, D).transpose(1, 0, 2)

    args = (
        image_counts, by_patch(images), by_patch(cotangent), w_tok_in.T, w_tok_out, w_up.T, w_down,
        norm_params, jnp.pad(biases, (0, NB_ROW - NB)).reshape(1, NB_ROW),
        root_right_up.T, root_left_down, root_left_up, root_right_down,
        right_up.T, left_down, left_up, right_down,
        root_left_tok_in, root_right_tok_in, root_left_tok_out, root_right_tok_out,
        left_tok_in, right_tok_in, left_tok_out, right_tok_out,
    )
    outs = [
        ((NX, PAIR, D), BF), ((NX, PAIR, D), BF), ((12, D), F32), ((12, D), F32), ((12, D), F32),
        ((12, D), F32), ((12, DC), F32), ((12, DC), F32), ((12, 192), F32), ((12, 192), F32),
        ((8, DS), F32), ((1, NB_ROW), F32), ((6, S), F32), ((6, S), F32), ((6, S), F32), ((6, S), F32),
        ((S, S), F32), ((DS, DS), F32), ((DS, DS), F32), ((S, S), F32),
    ]

    def shapes(items):
        return [jax.ShapeDtypeStruct(shape, dtype) for shape, dtype in items]

    def vm(dtype, *shape):
        return pltpu.VMEM(shape, dtype)

    copies = 400
    scratch = [
        pltpu.SemaphoreType.DMA((copies,)), pltpu.SemaphoreType.DMA((copies,)), pltpu.SemaphoreType.DMA((4,)),
        vm(F32, 32, DC), vm(BF, 32, D), vm(BF, 16, 256),
        *[vm(BF, NX, PAIR, D) for _ in range(4)],
        vm(BF, NX, 32, D), vm(BF, NY, NZ, 96, D), vm(BF, NY, NZ, 2, 16, 256),
        vm(BF, DS, 256), vm(BF, DS, 256), vm(F32, DS, 1), vm(F32, IMG, 1), vm(F32, 16, 1, 192),
        vm(F32, 2, IMG, D), vm(BF, 2, IMG, D), vm(F32, 2, IMG, D), vm(F32, 2, DS, D), vm(BF, 2, DS, D),
        vm(BF, 4 * ROW, D), vm(BF, 4 * ROW, D), vm(F32, 4 * ROW, D), vm(F32, 4 * ROW, D),
        vm(BF, D, D), vm(BF, D, D), vm(BF, 4 * ROW, 2 * D), vm(BF, 4 * ROW, 2 * D),
        vm(BF, 2, 2 * ROW, D),
        vm(BF, NY, NZ, 96, D),
        vm(BF, 4, NX, 96, 256), vm(BF, 3, NX, 96, 256), vm(BF, 3, 96, 256), vm(BF, 3, 48, TILE),
        vm(BF, 3, NZ, 96, 256), vm(BF, 3, NZ, NY, 48, TILE), vm(BF, 3, NZ, 48, TILE), vm(BF, 3, NZ, 48, TILE),
        vm(BF, NZ, 48, 256), vm(BF, 7, 48, 256),
        vm(BF, 2, NY, NZ, 48, DS), vm(BF, NY, 48, DS), vm(BF, 2, 80, D),
        vm(BF, 2, 16, DC), vm(BF, 2, NX, 16, D),
        vm(BF, NX, 2, 16, 1792), vm(BF, NX, 2, 16, 1792),
        vm(F32, 512, DS), vm(BF, NY, NZ, 16, DS), vm(BF, 3, NZ, 16, DS), vm(BF, 7, 16, DS),
        vm(BF, NY, 16, DS), vm(BF, 2, 16, DS), vm(BF, NY, NZ, 16, DS),
    ]
    in_vmem = pl.BlockSpec(memory_space=pltpu.VMEM)
    anywhere = pl.BlockSpec(memory_space=pl.ANY)
    rlay, rgrad, *rest = pl.pallas_call(
        fused,
        out_shape=shapes(outs),
        in_specs=[pl.BlockSpec(memory_space=pltpu.SMEM)]
        + [anywhere if i in (11, 12) else in_vmem for i in range(1, len(args))],
        out_specs=[anywhere, anywhere] + [in_vmem] * (len(outs) - 2),
        scratch_shapes=scratch,
        compiler_params=pltpu.CompilerParams(
            collective_id=0, has_side_effects=True, vmem_limit_bytes=64 * 2**20
        ),
        name="fused",
    )(*args)
    handed = rest[:8] + rest[10:]
    handed_outs = outs[2:10] + outs[12:]
    own_outs = [((patch_rows, D), BF), ((patch_rows, D), F32)] + [((4, D), F32)] * 3
    (
        gup, gdn, nup, ndn, rup, ldn, lup, rdn, gti, gto, nti, nto, lti, rti, lto, rto,
        layer, gimg, norm_grad, norm_second_new, norm_new,
    ) = pl.pallas_call(
        finish,
        out_shape=shapes(handed_outs + own_outs),
        in_specs=[in_vmem] * (5 + len(handed)),
        out_specs=[in_vmem] * (5 + len(handed)),
        compiler_params=pltpu.CompilerParams(vmem_limit_bytes=64 * 2**20),
        name="finish",
    )(rlay, rgrad, rest[8], norm_params, norm_second, *handed)

    bias_grad = rest[9].reshape(NB_ROW)[:NB]
    bias_second_new = 0.5 * bias_second + 0.5 * bias_grad * bias_grad
    bias_new = biases - 0.5 * bias_grad * lax.rsqrt(bias_second_new + 1e-08)
    return (
        by_image(layer), by_image(gimg), gti.T, gto, gup.T, gdn, nti.T, nto, nup.T, ndn,
        lti, rti, lto, rto, lup, rup.T, ldn, rdn,
        norm_grad, norm_second_new, norm_new, bias_grad, bias_second_new, bias_new,
    )


def solution(mesh):
    both, dp, rest = ("dp", "mix"), "dp", P()
    in_specs = (
        P(dp, "mix", None), P(dp, "mix", None), P(dp), P(None, dp), P(dp, None), P(None, both), P(both, None),
        rest, rest, rest, rest, rest, rest,
        P(dp, "mix"), P(None, both), P(both, None), P(dp, "mix"),
        rest, rest, rest, rest, rest, P(None, both), P(both, None), rest, rest, rest,
    )
    out_specs = (
        P(dp, "mix", None), P(dp, "mix", None), P(None, dp), P(dp, None), P(None, both), P(both, None),
        P(None, dp), P(dp, None), P(None, both), P(both, None),
        rest, rest, rest, rest, P(dp, "mix"), P(None, both), P(both, None), P(dp, "mix"),
        rest, rest, rest, rest, rest, rest,
    )
    return jax.shard_map(on_device, mesh=mesh, in_specs=in_specs, out_specs=out_specs, check_vma=False)
```

time: 193 us -> 157 us (0.81)
  local copies, waits for them, and re-layouts: 22.7 us -> 2.12 us
  Pallas kernels: 165 us -> 152 us
    unnamed x56 -> x2, local copies, waits for them, and re-layouts: 13.5 us -> 0.01 us
    pallas_call x1 -> x2, Pallas kernels: 165 us -> 152 us  [the longest x1 147 us: on_device(): pl.pallas_call(fused, out_shape=shapes(outs), in_specs=[pl.BlockSpec(memo...]
    slice x8 -> x1, local copies, waits for them, and re-layouts: 5.92 us -> 0.77 us  [on_device(): bias_grad = rest[9].reshape(NB_ROW)[:NB]]
    reshape x9 -> x0, local copies, waits for them, and re-layouts: 3.21 us -> none  [the longest x2 0.81 us: on_device(): biases[DS + S:DS + S + DC].reshape(NY, NZ, 2, 48).transpose(1, 2, 0, 3)]
where the time goes in v2:
time: 157 us
  Pallas kernels  152 us (97%)
  local copies, waits for them, and re-layouts  2.12 us (1%)
    pallas_call x1, Pallas kernels, on_device(): pl.pallas_call(fused, out_shape=shapes(outs), in_specs=[pl.BlockSpec(memo...  147 us
    pallas_call x1, Pallas kernels, on_device(): pl.pallas_call(finish, out_shape=shapes(handed_outs + own_outs), in_specs...  4.82 us

profile of v2, /device:TPU:1, one launch (start us, length us, event | category | flops | bytes accessed | tf_op | source)
XLA Modules:
  0.0 156.7 jit_solution(9697072271346348621)
XLA Ops:
  0.7 1.3 pad.4
  2.6 147.1 %fused.1 = (bf16[4,112,768]{2,1,0:T(8,128)(2,1)}, bf16[4,112,768]{2,1,0:T(8,128)(2,1)}, f32[12,768]{1,0:T(8,128)}, f32[12,768]{1,0:T(8,128)}, f32[12,768]{1,0:T(...) custom-call(s32[1]{0:T(128)S(6)} %copy.51.count, ...), custom_call_target="tpu_custom_call" | custom-call | tf_op jit(solution)/shard_map/fused/pallas_call | solution.py:814
  149.7 4.8 %finish.1 = (f32[12,768]{1,0:T(8,128)}, f32[12,768]{1,0:T(8,128)}, f32[12,768]{1,0:T(8,128)}, f32[12,768]{1,0:T(8,128)}, f32[12,3072]{1,0:T(8,128)}, /*index=5*/...) custom-call(bf16[4,112,768]{2,1,0:T(8,128)(2,1)} %get-tuple-element., ...), custom_call_target="tpu_custom_call" | custom-call | tf_op jit(solution)/shard_map/finish/pallas_call | solution.py:832
  154.6 0.8 slice_reduce_fusion
  155.3 0.0 copy-start
  155.4 1.4 fusion.1
  156.7 0.0 copy-done
Async XLA Ops:
  155.3 1.4 copy-start

commit v3 on v2

--- a/solution.py
+++ b/solution.py
@@ -18,15 +18,16 @@
 EPS = 1e-06
 PER_IMAGE = 1.0 / 512.0
 PATCHES = 49
+NUM_LATE = 16
 PAIR = 112
 IMG = 256
 ROW = 208
 HALF = D // 2
 NB = 4420
-NB_ROW = 5120
 TILE = 128
 P0, P1, P2 = slice(0, 256), slice(256, 512), slice(512, 768)
 FAR_FIRST = (4, 5, 3, 6, 2, 7, 1, 0)
+NEAR, FAR = (0, 7, 1, 2), (6, 3, 5, 4)
 
 
 def dot(left, right, left_dim=1, right_dim=0, precision=None):
@@ -75,16 +76,23 @@
 
 
 def fused(
-    count, img, cot, tin, tout, wup, wdn, norm, bias,
-    q_up, p_dn, p_up, q_dn, old_r_up, old_l_dn, old_l_up, old_r_dn,
-    pl_ti, pr_ti, pl_to, pr_to, ol_ti, or_ti, ol_to, or_to,
-    rlay, rgrad, o_gup, o_gdn, o_nup, o_ndn, o_rup, o_ldn, o_lup, o_rdn,
-    o_norm, o_bias, o_gti, o_gto, o_nti, o_nto, o_lti, o_rti, o_lto, o_rto,
-    ssem, rsem, lsem, stage, wst, tst, simg, scot, rimg, rcot,
-    xw, W, tk, tokin, tokout, bti, bto, bup, ximg, normed, mid, slope, act, n2, mb, br, dn,
-    upc, dnc, actb, dpb, xbi, G, RAr, RAl, XA, YA, XB, YB, YC, XD, PZ, RZ,
-    HQ, UJQ, UJP, qst, Qx, XEo, XEi, SM, SB, SX, SZ, SY, SC, SF,
+    count, img, cot_far, tin, tout, wup, wdn, norm, bias, *refs
 ):
+    late = refs[:NUM_LATE]
+    (
+        rlay, rgrad, o_gup, o_gdn, o_nup, o_ndn, o_rup, o_ldn, o_lup, o_rdn,
+        o_norm, o_bias, o_gti, o_gto, o_nti, o_nto, o_lti, o_rti, o_lto, o_rto,
+        ssem, rsem, lsem, stage, wst, tst, simg, scot, rimg, rcot,
+        xw, W, tk, tokin, tokout, bti, bto, bup, brow, ximg, normed, mid, slope, act, n2, mb, br, dn,
+        upc, dnc, actb, dpb, xbi, G, RAr, RAl, XA, YA, XB, YB, YC, XD, PZ, RZ,
+        HQ, UJQ, UJP, qst, Qx, XEo, XEi, SM, SB, SX, SZ, SY, SC, SF,
+        cot, q_up, p_dn, old_r_up, old_l_dn, old_l_up, old_r_dn,
+        pl_ti, pr_ti, pl_to, pr_to, ol_ti, or_ti, ol_to, or_to,
+    ) = refs[NUM_LATE:]
+    loaded = (
+        q_up, p_dn, None, None, old_r_up, old_l_dn, old_l_up, old_r_dn,
+        pl_ti, pr_ti, pl_to, pr_to, ol_ti, or_ti, ol_to, or_to,
+    )
     dp = lax.axis_index("dp")
     x = lax.axis_index("mix")
     c = lax.rem(dp, 2)
@@ -141,6 +149,13 @@
     for peer in peers:
         pl.semaphore_signal(barrier, inc=1, device_id=peer, device_id_type=MESH)
 
+    get_cot = pltpu.make_async_copy(cot_far, cot, lsem.at[0])
+    get_cot.start()
+    loads = [None] * NUM_LATE
+    for k in (0, 1, *range(4, NUM_LATE)):
+        loads[k] = pltpu.make_async_copy(late[k], loaded[k], lsem.at[4 + k])
+        loads[k].start()
+
     stage[:, 0 : 2 * D] = jnp.zeros((32, 2 * D), F32)
     stage[0:12, 0:D] = wup[...]
     stage[16:28, 0:D] = wdn[...]
@@ -153,7 +168,7 @@
 
     pl.semaphore_wait(barrier, len(peers))
     c_xw = [put(wst, xw.at[x], to_x[i]) for i in range(1, NX)]
-    c_ty = [put(tk.at[y, z, c], tk.at[y, z, c], to_y[i]) for i in range(1, NY)]
+    c_tz = [put(tk.at[y, z, c], tk.at[y, z, c], to_z[i]) for i in range(1, NZ)]
 
     def of_pairs(row, col):
         m = ge(row, PAIR) + ge(row, 2 * PAIR) + ge(row, 3 * PAIR)
@@ -164,6 +179,9 @@
     chooser = pick(NX * PAIR, 8 * PATCHES, of_pairs)
     simg[...] = dot(chooser, img[...]).astype(BF).reshape(NX, PAIR, D)
     c_img = [put(simg.at[X(i)], rimg.at[x], to_x[i]) for i in range(1, NX)]
+    get_cot.wait()
+    scot[...] = dot(chooser, cot[...]).astype(BF).reshape(NX, PAIR, D)
+    c_cot = [put(scot.at[X(i)], rcot.at[x], to_x[i]) for i in range(1, NX)]
 
     arrived(c_xw)
 
@@ -207,55 +225,49 @@
     def c_ref(yy, zz):
         return W.at[yy, zz, rows_of(x), lanes_of(x, 2)]
 
-    def c_spread(d):
-        ref = c_ref(Y(-d), slice(None))
-        return [put(ref, ref, to_x[i]) for i in range(1, NX)]
+    def c_part(k, i):
+        return W.at[:, Z(k), rows_of(X(i)), lanes_of(X(i), 2)]
 
     W[y, z, rows_of(x), lanes_of(x, 2)] = upc[rows_of(x), lanes_of(x, 2)]
     own_a = W.at[y, z, :, P0]
+    def c_send_y(k):
+        ref = c_ref(y, Z(k))
+        c_y[k] = [put(ref, ref, to_y[i]) for i in range(1, NY)]
+
+    c_z, c_y = {}, {}
+    for i in (1, 7, 6, 2, 5, 3, 4):
+        c_z[i] = put(c_ref(y, z), c_ref(y, z), to_z[i])
     b_send(1, True)
     b_send(1, False)
     c_ay = [None] + [put(own_a, own_a, to_y[i]) for i in range(1, NY)]
-    c_cz = [put(c_ref(y, z), c_ref(y, z), to_z[i]) for i in range(1, NZ)]
-    arrived(c_ty)
-    c_tz = [put(tk.at[:, z, c], tk.at[:, z, c], to_z[i]) for i in range(1, NZ)]
+    c_send_y(0)
     a_send(1, 0, True)
     a_send(1, 0, False)
     b_spread(0)
+
+    rimg[x] = simg[x]
+    rcot[x] = scot[x]
+    diagonal = pick(TILE, TILE, lambda row, col: row == col).astype(F32)
+    brow[...] = bias[...].reshape(1, NB)
+
+    def column(first):
+        spread = jnp.broadcast_to(brow[:, first : first + TILE], (TILE, TILE))
+        return jnp.sum(spread * diagonal, axis=1, keepdims=True)
+
+    for j in range(3):
+        bti[TILE * j : TILE * j + TILE, :] = column(TILE * j)
+    for j in range(2):
+        bto[TILE * j : TILE * j + TILE, :] = column(DS + TILE * j)
     for d in (1, 3, 2):
         c_ay[d].wait_recv()
         a_send(1, d, True)
         a_send(1, d, False)
-
-    scot[...] = dot(chooser, cot[...]).astype(BF).reshape(NX, PAIR, D)
-    c_cot = [put(scot.at[X(i)], rcot.at[x], to_x[i]) for i in range(1, NX)]
-    rimg[x] = simg[x]
-    rcot[x] = scot[x]
-    stage[0:12, :] = q_up[...]
-    stage[12:16, :] = jnp.zeros((4, DC), F32)
-    stage[16:28, :] = p_dn[...]
-    stage[28:32, :] = jnp.zeros((4, DC), F32)
-    qst[0] = stage[0:16, :].astype(BF)
-    qst[1] = stage[16:32, :].astype(BF)
-    diagonal = pick(TILE, TILE, lambda row, col: row == col).astype(F32)
-
-    def column(first):
-        spread = jnp.broadcast_to(bias[:, first : first + TILE], (TILE, TILE))
-        return jnp.sum(spread * diagonal, axis=1, keepdims=True)
-
-    for j in range(3):
-        bti[TILE * j : TILE * j + TILE, :] = column(TILE * j)
-    for j in range(2):
-        bto[TILE * j : TILE * j + TILE, :] = column(DS + TILE * j)
-    for zz in range(NZ):
-        for cc in range(2):
-            first = [DS + S + 48 * ((yy * NZ + zz) * 2 + cc) for yy in range(NY)]
-            bup[2 * zz + cc] = jnp.concatenate([bias[:, f : f + 48] for f in first], axis=1)
-    bias_down = bias[:, DS + S + DC : NB]
-
-    arrived(c_cz)
-    c_cy = [None] + [put(c_ref(y, slice(None)), c_ref(y, slice(None)), to_y[i]) for i in range(1, NY)]
-    c_cx = c_spread(0)
+    arrived(c_tz)
+    c_ty = [put(tk.at[y, :, c], tk.at[y, :, c], to_y[i]) for i in range(1, NY)]
+    x_right, x_left, x_on, x_far = {}, {}, {}, []
+    for k in NEAR[1:]:
+        c_z[NZ - k].wait_recv()
+        c_send_y(k)
 
     def gather_step(step):
         b_right[step].wait_recv()
@@ -267,20 +279,31 @@
             if step < 3:
                 b_send(step + 1, False)
             b_spread(step)
-        for d in (0, 1, 3, 2):
-            a_right[step, d].wait_recv()
-            if step < 4:
-                a_send(step + 1, d, True)
+        if step < 4:
+            for d in (0, 1, 3, 2):
+                a_right[step, d].wait_recv()
+                if step < 3 or d < 2:
+                    a_send(step + 1, d, True)
                 a_left[step, d].wait_recv()
-                if step < 3:
+                if step < 3 or d > 1:
                     a_send(step + 1, d, False)
 
-    arrived(c_tz)
+    gather_step(1)
+    for k in FAR:
+        c_z[NZ - k].wait_recv()
+        c_send_y(k)
+    arrived(c_ty)
     c_tc = put(tk.at[:, :, c], tk.at[:, :, c], sibling)
-    gather_step(1)
-    for d in (1, 3, 2):
-        c_cy[d].wait_recv()
-        c_cx = c_cx + c_spread(d)
+    for k in NEAR:
+        arrived(c_y[k])
+        x_right[k] = put(c_part(k, 0), c_part(k, 0), to_x[1])
+        x_left[k] = put(c_part(k, 0), c_part(k, 0), to_x[3])
+    for zz in range(NZ):
+        for cc in range(2):
+            first = [DS + S + 48 * ((yy * NZ + zz) * 2 + cc) for yy in range(NY)]
+            bup[2 * zz + cc] = jnp.concatenate([brow[:, f : f + 48] for f in first], axis=1)
+    bias_down = brow[:, DS + S + DC : NB]
+
     c_tc.wait_recv()
 
     def of_group(row, col):
@@ -320,6 +343,9 @@
         xhat, _ = normalise(ximg[b])
         normed[b] = (xhat * norm[0:1, :] + norm[1:2, :]).astype(BF)
     c_mb = put(mb.at[both], mb.at[both], sibling)
+    for k in FAR:
+        arrived(c_y[k])
+        x_far += [put(c_part(k, 0), c_part(k, 0), to_x[i]) for i in range(1, NX)]
     gather_step(2)
 
     @pl.loop(0, 2)
@@ -335,17 +361,19 @@
         n2[own_rows(b), :] = (xhat * norm[2:3, :] + norm[3:4, :]).astype(BF)
 
     c_n2 = put(n2.at[both], n2.at[both], sibling)
+    for k in NEAR:
+        if k < 2:
+            x_right[k].wait_recv()
+            x_on[k] = put(c_part(k, 3), c_part(k, 3), to_x[1])
+        else:
+            x_left[k].wait_recv()
+            x_on[k] = put(c_part(k, 1), c_part(k, 1), to_x[3])
     gather_step(3)
     gather_step(4)
-    for offset in (0, -1, 1, -2, 2, -3, 3, -4):
-        arrived(b_y[offset])
-    arrived(c_cx)
     c_mb.wait_recv()
     c_n2.wait_recv()
 
-    br[...] = jnp.zeros_like(br)
-    dn[...] = jnp.zeros_like(dn)
-    for half in range(2):
+    def channel_pass(half):
         offsets = FAR_FIRST[4 * half : 4 * half + 4]
         for j, k in enumerate(offsets):
             upc[192 * j : 192 * j + 192, :] = W[:, Z(k), 0:48, :].reshape(192, D)
@@ -353,23 +381,19 @@
         row = jnp.concatenate([bup[2 * Z(k) + c] for k in offsets], axis=1)
         lanes = slice(half * D, half * D + D)
 
-        @pl.loop(0, 4)
-        def _(r, row=row, lanes=lanes):
-            rows = pl.ds(pl.multiple_of(r * ROW, 16), ROW)
+        @pl.loop(0, 2)
+        def _(r):
+            rows = pl.ds(pl.multiple_of(r * (2 * ROW), 16), 2 * ROW)
             pre = dot(n2[rows, :], upc[...], 1, 1) + row
             value, grad = gelu_and_slope(pre)
             low = value.astype(BF)
             actb[rows, lanes] = low
-            br[rows, :] += dot(low, dnc[...])
+            part = dot(low, dnc[...])
+            br[rows, :] = part if half == 1 else br[rows, :] + part
             low = (grad * dot(mb[rows, :], dnc[...], 1, 1)).astype(BF)
             dpb[rows, lanes] = low
-            dn[rows, :] += dot(low, upc[...])
-
-    other = pl.ds(pl.multiple_of((1 - c) * (2 * ROW), 16), 2 * ROW)
-    upc[0 : 2 * ROW, :] = dn[other, :].astype(BF)
-    c_dn = put(upc.at[0 : 2 * ROW], xbi.at[1], sibling)
-    dnc[0 : 2 * ROW, :] = br[other, :].astype(BF)
-    c_br = put(dnc.at[0 : 2 * ROW], xbi.at[0], sibling)
+            part = dot(low, upc[...])
+            dn[rows, :] = part if half == 1 else dn[rows, :] + part
 
     ra, la, xb, yb, yc, xd, rz = {}, {}, {}, {}, {}, {}, {}
 
@@ -387,16 +411,19 @@
                 ref = G.at[:, Z(k), rows_of(Y(i)), lanes_of(Y(i), 2)]
                 yb[k, i] = put(ref, YB.at[i - 1, Z(k)], to_y[i])
 
-    def a_reduce(step):
-        for w in range(NX):
-            ref = G.at[X(w), Z(5 - step), :, P0]
-            if step > 1:
-                ra[step - 1, w].wait_recv()
-                ref[...] = total(ref[...], RAr[step - 2, w]).astype(BF)
-            ra[step, w] = put(ref, RAr.at[step - 1, w], to_z[1])
-            if step < 4:
-                ref = G.at[X(w), Z(step - 4), :, P0]
-                if step > 1:
+    def a_reduce(step, ws):
+        for w in ws:
+            first = 1 if w < 2 else 2
+            if step >= first:
+                ref = G.at[X(w), Z(5 - step), :, P0]
+                if step > first:
+                    ra[step - 1, w].wait_recv()
+                    ref[...] = total(ref[...], RAr[step - 2, w]).astype(BF)
+                ra[step, w] = put(ref, RAr.at[step - 1, w], to_z[1])
+            first = 2 if w < 2 else 1
+            if step >= first:
+                ref = G.at[X(w), Z(step - 5), :, P0]
+                if step > first:
                     la[step - 1, w].wait_recv()
                     ref[...] = total(ref[...], RAl[step - 2, w]).astype(BF)
                 la[step, w] = put(ref, RAl.at[step - 1, w], to_z[7])
@@ -425,21 +452,53 @@
         if k > 0:
             rz[k] = put(PZ.at[Z(k)], RZ.at[k - 1], to_z[k])
 
+    for offset in (0, -1, 1, 2):
+        arrived(b_y[offset])
+    for k in NEAR:
+        arrived([x_left[k] if k < 2 else x_right[k], x_on[k]])
+    loads[0].wait()
+    loads[1].wait()
+    stage[0:12, :] = q_up[...]
+    stage[12:16, :] = jnp.zeros((4, DC), F32)
+    stage[16:28, :] = p_dn[...]
+    stage[28:32, :] = jnp.zeros((4, DC), F32)
+    qst[0] = stage[0:16, :].astype(BF)
+    qst[1] = stage[16:32, :].astype(BF)
+    Qx[:, x] = qst[:, :, pl.ds(pl.multiple_of(x * D, D), D)]
+    c_q = [
+        put(qst.at[:, :, pl.ds(pl.multiple_of(X(i) * D, D), D)], Qx.at[:, x], to_x[i])
+        for i in range(1, NX)
+    ]
+    channel_pass(1)
+    gradients(2)
+    gradients(3)
+    for offset in (-2, 3, -3, -4):
+        arrived(b_y[offset])
+    arrived(x_far)
+    for d in (0, 1, 3, 2):
+        (a_right if d < 2 else a_left)[4, d].wait_recv()
+    channel_pass(0)
+
+    other = pl.ds(pl.multiple_of((1 - c) * (2 * ROW), 16), 2 * ROW)
+    upc[0 : 2 * ROW, :] = dn[other, :].astype(BF)
+    c_dn = put(upc.at[0 : 2 * ROW], xbi.at[1], sibling)
+    dnc[0 : 2 * ROW, :] = br[other, :].astype(BF)
+    c_br = put(dnc.at[0 : 2 * ROW], xbi.at[0], sibling)
+
     gradients(0)
-    a_reduce(1)
+    a_reduce(1, range(4))
     gradients(1)
-    gradients(2)
-    a_reduce(2)
-    gradients(3)
-
-    c_dn.wait_recv()
-    c_br.wait_recv()
+    for k in NEAR:
+        second(k)
+
     ones = jnp.ones((8, 4 * ROW), BF)
     up_sums = dot(ones, dpb[...])[0:1]
     down_sums = dot(ones[:, 0 : 2 * ROW], mb[both, :])
     lob, dmx = actb, dpb
     lob[0 : 2 * IMG, 0:D] = jnp.zeros((2 * IMG, D), BF)
     dmx[0 : 2 * IMG, 0:D] = jnp.zeros((2 * IMG, D), BF)
+    c_dn.wait_recv()
+    c_br.wait_recv()
     gain_two = jnp.zeros((1, D), F32)
     shift_two = jnp.zeros((1, D), F32)
     for b in range(2):
@@ -454,6 +513,7 @@
         back = mb[own_rows(b), :].astype(F32) + dv
         mid[b, 0:ROW] = back
         dmx[b * IMG : b * IMG + ROW, 0:D] = back.astype(BF)
+        a_reduce(2, (2 * b, 2 * b + 1))
 
     def of_out(row, col):
         m = ge(row, PAIR) + ge(row, 2 * PAIR) + ge(row, 3 * PAIR)
@@ -468,19 +528,13 @@
         settle(sent)
         buffer[...] = dot(out_chooser, lob[0 : 2 * IMG, 0:D]).astype(BF).reshape(NX, PAIR, D)
 
-    second(4)
-    second(5)
-    a_reduce(3)
+    a_reduce(3, (0, 1))
     to_patches(simg, c_img)
-    own_out = [pltpu.make_async_copy(simg.at[x], rlay.at[x], lsem.at[2])]
-    own_out[0].start()
-    c_lay = [put(simg.at[X(i)], rlay.at[x], to_x[i]) for i in range(1, NX)]
-    second(3)
-    second(6)
+    a_reduce(3, (2, 3))
 
     roots = [
-        pltpu.make_async_copy(p_up, br.at[0:D], lsem.at[0]),
-        pltpu.make_async_copy(q_dn, dn.at[0:D], lsem.at[1]),
+        pltpu.make_async_copy(late[2], br.at[0:D], lsem.at[0]),
+        pltpu.make_async_copy(late[3], dn.at[0:D], lsem.at[1]),
     ]
     for copy in roots:
         copy.start()
@@ -505,16 +559,23 @@
         shift_one = shift_one + shift
         lob[b * IMG : b * IMG + ROW, 0:D] = (mid[b, 0:ROW] + dv).astype(BF)
         if b == 0:
-            a_reduce(4)
-            second(2)
-            second(7)
-            third(4)
-            third(5)
-        else:
-            second(1)
-            second(0)
-            third(3)
-            third(6)
+            a_reduce(4, (0, 1))
+            second(4)
+            second(5)
+            a_reduce(4, (2, 3))
+
+    second(3)
+    second(6)
+    c_xa = []
+    for w in (1, 3, 2, 0):
+        ra[4, w].wait_recv()
+        la[4, w].wait_recv()
+        ref = G.at[X(w), z, :, P0]
+        ref[...] = total(ref[...], RAr[3, w], RAl[3, w]).astype(BF)
+        if w > 0:
+            c_xa.append(put(ref, XA.at[w - 1], to_x[w]))
+    for k in NEAR:
+        third(k)
 
     SM[0:IMG, :] = gti
     SM[IMG : IMG + ROW, :] = gto[0:ROW]
@@ -532,15 +593,7 @@
     SB[...] = SM[...].reshape(NY, NZ, 16, DS).astype(BF)
     c_sx = [put(SB.at[X(i)], SX.at[i - 1], to_x[i]) for i in range(1, NX)]
 
-    c_xa = []
-    for w in (1, 3, 2, 0):
-        ra[4, w].wait_recv()
-        la[3, w].wait_recv()
-        ref = G.at[X(w), z, :, P0]
-        ref[...] = total(ref[...], RAr[3, w], RAl[2, w]).astype(BF)
-        if w > 0:
-            c_xa.append(put(ref, XA.at[w - 1], to_x[w]))
-    for k in (2, 7, 1, 0):
+    for k in (4, 5):
         third(k)
     arrived(c_xa)
     ref = G.at[x, z, :, P0]
@@ -549,19 +602,28 @@
         put(G.at[x, z, rows_of(Y(i)), lanes_of(Y(i), 0)], YA.at[i - 1], to_y[i])
         for i in range(1, NY)
     ]
+    for k in (3, 6):
+        third(k)
     arrived(c_sx)
     SB[x] = total(SB[x], SX[0], SX[1], SX[2]).astype(BF)
     c_sz = [put(SB.at[x, Z(i)], SZ.at[i - 1], to_z[i]) for i in range(1, NZ)]
 
+
+    hz, hy, hs = {}, {}, {}
+
+    def h_send(lanes):
+        ref = HQ.at[c, y, z, :, lanes]
+        for i in (4, 3, 5, 2, 6, 1, 7):
+            hz[i] = hz.get(i, []) + [put(ref, ref, to_z[i])]
+
+    arrived(c_ya)
+    mean = total(G[x, z, rows_of(y), lanes_of(y, 0)], YA[0], YA[1], YA[2]) * PER_IMAGE
+    HQ[c, y, z, :, 0:TILE] = mean.astype(BF)
+    h_send(slice(0, TILE))
     arrived(rz.values())
     mean = total(PZ[z], *[RZ[i] for i in range(NZ - 1)]) * PER_IMAGE
     HQ[c, y, z, :, TILE:] = mean.astype(BF)
-    arrived(c_ya)
-    mean = total(G[x, z, rows_of(y), lanes_of(y, 0)], YA[0], YA[1], YA[2]) * PER_IMAGE
-    HQ[c, y, z, :, 0:TILE] = mean.astype(BF)
-    hz, hy, hs = {}, {}, {}
-    for i in (4, 3, 5, 2, 6, 1, 7):
-        hz[i] = put(HQ.at[c, y, z], HQ.at[c, y, z], to_z[i])
+    h_send(slice(TILE, DS))
 
     def h_spread(offset):
         ref = HQ.at[c, y, Z(offset)]
@@ -573,6 +635,9 @@
         hs[offset] = put(ref, ref, sibling)
 
     h_spread(0)
+    own_out = [pltpu.make_async_copy(simg.at[x], rlay.at[x], lsem.at[2])]
+    own_out[0].start()
+    c_lay = [put(simg.at[X(i)], rlay.at[x], to_x[i]) for i in range(1, NX)]
     to_patches(scot, c_cot)
     own_out.append(pltpu.make_async_copy(scot.at[x], rgrad.at[x], lsem.at[3]))
     own_out[1].start()
@@ -581,7 +646,7 @@
     SY[y] = total(SB[x, z], *[SZ[i] for i in range(NZ - 1)]).astype(BF)
     c_sy = [put(SY.at[y], SY.at[y], to_y[i]) for i in range(1, NY)]
     for i in (1, 7, 2, 6):
-        hz[i].wait_recv()
+        arrived(hz[i])
         h_spread(-i)
     h_share(0)
 
@@ -604,19 +669,13 @@
     SC[c] = total(SY[0], SY[1], SY[2], SY[3]).astype(BF)
     c_sc = put(SC.at[c], SC.at[c], sibling)
     for i in (3, 5, 4):
-        hz[i].wait_recv()
+        arrived(hz[i])
         h_spread(-i)
     c_sc.wait_recv()
     SF[x, z] = (total(SC[0], SC[1]) * PER_IMAGE).astype(BF)
     c_fz = [put(SF.at[x, z], SF.at[x, z], to_z[i]) for i in range(1, NZ)]
     for i in (1, 7, 2, 6):
         h_share(-i)
-    Qx[:, x] = qst[:, :, pl.ds(pl.multiple_of(x * D, D), D)]
-    c_q = [
-        put(qst.at[:, :, pl.ds(pl.multiple_of(X(i) * D, D), D)], Qx.at[:, x], to_x[i])
-        for i in range(1, NX)
-    ]
-
     @pl.when(x != y)
     def _():
         j_copy(1).wait_recv()
@@ -648,6 +707,7 @@
 
     arrived([hs[offset] for offset in (0, -1, -7, -2, -6, -3, -5, -4)])
     arrived(c_q)
+    c_xe = []
     for u in range(2):
         store = (n2, mb)[u]
         for zz in range(NZ):
@@ -663,8 +723,11 @@
             XEo[m, u, :, D : 2 * D] = left[16 * m : 16 * m + 16].astype(BF)
             XEo[m, u, :, 2 * D : 2 * D + 192] = left[64:80, 192 * m : 192 * m + 192].astype(BF)
             XEo[m, u, :, 2 * D + 192 : 2 * D + 256] = jnp.zeros((16, 64), BF)
-    XEi[x] = XEo[x]
-    c_xe = [put(XEo.at[X(i)], XEi.at[x], to_x[i]) for i in range(1, NX)]
+        XEi[x, u] = XEo[x, u]
+        c_xe.append([put(XEo.at[X(i), u], XEi.at[x, u], to_x[i]) for i in range(1, NX)])
+
+    for copy in loads[4:]:
+        copy.wait()
 
     arrived(c_fx)
     small = SF[...].reshape(512, DS)
@@ -676,7 +739,7 @@
         for zz in range(NZ):
             for cc in range(2):
                 pieces.append(ups[8 * cc + zz : 8 * cc + zz + 1, 48 * yy : 48 * yy + 48])
-    pieces += [vector[24:25], vector[32:33], jnp.zeros((1, NB_ROW - NB), F32)]
+    pieces += [vector[24:25], vector[32:33]]
     o_bias[...] = jnp.concatenate(pieces, axis=1)
     real = lax.broadcasted_iota(jnp.int32, (IMG, DS), 0) < S
     g_in = jnp.where(real, small[0:IMG].astype(F32), 0.0).astype(BF)
@@ -698,13 +761,16 @@
     step = dot(step, pr_to[...], 1, 0, HIGH)
     o_nto[...] = tout[...] - 0.5 * step[0:6]
 
-    arrived(c_xe)
     for copy in roots:
         copy.wait()
+    settle([c_br])
+    upc[...] = br[0:D, :].astype(BF)
+    dnc[...] = dn[0:D, :].astype(BF)
     for u, (o_stat, old_stat, o_side, old_side, o_new, weight, root, dim) in enumerate((
-        (o_rup, old_r_up, o_lup, old_l_up, o_nup, wup, br, 1),
-        (o_ldn, old_l_dn, o_rdn, old_r_dn, o_ndn, wdn, dn, 0),
+        (o_rup, old_r_up, o_lup, old_l_up, o_nup, wup, upc, 1),
+        (o_ldn, old_l_dn, o_rdn, old_r_dn, o_ndn, wdn, dnc, 0),
     )):
+        arrived(c_xe[u])
         for m in range(NX):
             lanes = slice(D * m, D * m + D)
             fresh = XEi[m, u, :, 0:D][0:12].astype(F32)
@@ -712,8 +778,10 @@
         side = total(*[XEi[m, u, :, 2 * D : 2 * D + 192] for m in range(NX)])
         o_side[...] = 0.5 * old_side[...] + 0.5 * side[0:12]
         step = total(*[XEi[m, u, :, D : 2 * D] for m in range(NX)])
-        step = dot(step, root[0:D, :], 1, dim, HIGH)
-        o_new[...] = weight[...] - 0.5 * step[0:12]
+        high = step.astype(BF)
+        step = jnp.concatenate([high, (step - high.astype(F32)).astype(BF)], axis=0)
+        step = dot(step, root[...], 1, dim)
+        o_new[...] = weight[...] - 0.5 * (step[0:12] + step[16:28])
 
     arrived(c_lay)
     arrived(c_grad)
@@ -728,11 +796,11 @@
 
 
 def finish(
-    rlay, rgrad, grads, norm, second, *refs
+    rlay, rgrad, grads, bias_grad, norm, second, bias, bias_second, *refs
 ):
-    handed = (len(refs) - 5) // 2
+    handed = (len(refs) - 8) // 2
     sources, outs = refs[:handed], refs[handed:]
-    o_layer, o_gimg, o_grad, o_second, o_norm = outs[handed:]
+    o_layer, o_gimg, o_grad, o_second, o_norm, o_bias_grad, o_bias_second, o_bias = outs[handed:]
     for src, dst in zip(sources, outs):
         dst[...] = src[...]
 
@@ -751,6 +819,11 @@
         o_grad[row, :] = grad
         o_second[row, :] = fresh
         o_norm[row, :] = norm[row, :] - 0.5 * grad * lax.rsqrt(fresh + 1e-08)
+    grad = bias_grad[...].reshape(NB)
+    fresh = 0.5 * bias_second[...] + 0.5 * grad * grad
+    o_bias_grad[...] = grad
+    o_bias_second[...] = fresh
+    o_bias[...] = bias[...] - 0.5 * grad * lax.rsqrt(fresh + 1e-08)
 
 
 def on_device(
@@ -769,7 +842,7 @@
 
     args = (
         image_counts, by_patch(images), by_patch(cotangent), w_tok_in.T, w_tok_out, w_up.T, w_down,
-        norm_params, jnp.pad(biases, (0, NB_ROW - NB)).reshape(1, NB_ROW),
+        norm_params, biases,
         root_right_up.T, root_left_down, root_left_up, root_right_down,
         right_up.T, left_down, left_up, right_down,
         root_left_tok_in, root_right_tok_in, root_left_tok_out, root_right_tok_out,
@@ -778,7 +851,7 @@
     outs = [
         ((NX, PAIR, D), BF), ((NX, PAIR, D), BF), ((12, D), F32), ((12, D), F32), ((12, D), F32),
         ((12, D), F32), ((12, DC), F32), ((12, DC), F32), ((12, 192), F32), ((12, 192), F32),
-        ((8, DS), F32), ((1, NB_ROW), F32), ((6, S), F32), ((6, S), F32), ((6, S), F32), ((6, S), F32),
+        ((8, DS), F32), ((1, NB), F32), ((6, S), F32), ((6, S), F32), ((6, S), F32), ((6, S), F32),
         ((S, S), F32), ((DS, DS), F32), ((DS, DS), F32), ((S, S), F32),
     ]
 
@@ -790,17 +863,17 @@
 
     copies = 400
     scratch = [
-        pltpu.SemaphoreType.DMA((copies,)), pltpu.SemaphoreType.DMA((copies,)), pltpu.SemaphoreType.DMA((4,)),
+        pltpu.SemaphoreType.DMA((copies,)), pltpu.SemaphoreType.DMA((copies,)), pltpu.SemaphoreType.DMA((4 + NUM_LATE,)),
         vm(F32, 32, DC), vm(BF, 32, D), vm(BF, 16, 256),
         *[vm(BF, NX, PAIR, D) for _ in range(4)],
         vm(BF, NX, 32, D), vm(BF, NY, NZ, 96, D), vm(BF, NY, NZ, 2, 16, 256),
-        vm(BF, DS, 256), vm(BF, DS, 256), vm(F32, DS, 1), vm(F32, IMG, 1), vm(F32, 16, 1, 192),
+        vm(BF, DS, 256), vm(BF, DS, 256), vm(F32, DS, 1), vm(F32, IMG, 1), vm(F32, 16, 1, 192), vm(F32, 1, NB),
         vm(F32, 2, IMG, D), vm(BF, 2, IMG, D), vm(F32, 2, IMG, D), vm(F32, 2, DS, D), vm(BF, 2, DS, D),
         vm(BF, 4 * ROW, D), vm(BF, 4 * ROW, D), vm(F32, 4 * ROW, D), vm(F32, 4 * ROW, D),
         vm(BF, D, D), vm(BF, D, D), vm(BF, 4 * ROW, 2 * D), vm(BF, 4 * ROW, 2 * D),
         vm(BF, 2, 2 * ROW, D),
         vm(BF, NY, NZ, 96, D),
-        vm(BF, 4, NX, 96, 256), vm(BF, 3, NX, 96, 256), vm(BF, 3, 96, 256), vm(BF, 3, 48, TILE),
+        vm(BF, 4, NX, 96, 256), vm(BF, 4, NX, 96, 256), vm(BF, 3, 96, 256), vm(BF, 3, 48, TILE),
         vm(BF, 3, NZ, 96, 256), vm(BF, 3, NZ, NY, 48, TILE), vm(BF, 3, NZ, 48, TILE), vm(BF, 3, NZ, 48, TILE),
         vm(BF, NZ, 48, 256), vm(BF, 7, 48, 256),
         vm(BF, 2, NY, NZ, 48, DS), vm(BF, NY, 48, DS), vm(BF, 2, 80, D),
@@ -808,6 +881,9 @@
         vm(BF, NX, 2, 16, 1792), vm(BF, NX, 2, 16, 1792),
         vm(F32, 512, DS), vm(BF, NY, NZ, 16, DS), vm(BF, 3, NZ, 16, DS), vm(BF, 7, 16, DS),
         vm(BF, NY, 16, DS), vm(BF, 2, 16, DS), vm(BF, NY, NZ, 16, DS),
+        vm(BF, patch_rows, D), vm(F32, 12, DC), vm(F32, 12, DC), vm(F32, 12, DC), vm(F32, 12, DC),
+        vm(F32, 12, 192), vm(F32, 12, 192),
+        *[vm(F32, n, n) for n in (S, DS, DS, S, S, DS, DS, S)],
     ]
     in_vmem = pl.BlockSpec(memory_space=pltpu.VMEM)
     anywhere = pl.BlockSpec(memory_space=pl.ANY)
@@ -815,7 +891,7 @@
         fused,
         out_shape=shapes(outs),
         in_specs=[pl.BlockSpec(memory_space=pltpu.SMEM)]
-        + [anywhere if i in (11, 12) else in_vmem for i in range(1, len(args))],
+        + [anywhere if i == 2 or i > 8 else in_vmem for i in range(1, len(args))],
         out_specs=[anywhere, anywhere] + [in_vmem] * (len(outs) - 2),
         scratch_shapes=scratch,
         compiler_params=pltpu.CompilerParams(
@@ -825,22 +901,19 @@
     )(*args)
     handed = rest[:8] + rest[10:]
     handed_outs = outs[2:10] + outs[12:]
-    own_outs = [((patch_rows, D), BF), ((patch_rows, D), F32)] + [((4, D), F32)] * 3
+    own_outs = [((patch_rows, D), BF), ((patch_rows, D), F32)] + [((4, D), F32)] * 3 + [((NB,), F32)] * 3
     (
         gup, gdn, nup, ndn, rup, ldn, lup, rdn, gti, gto, nti, nto, lti, rti, lto, rto,
-        layer, gimg, norm_grad, norm_second_new, norm_new,
+        layer, gimg, norm_grad, norm_second_new, norm_new, bias_grad, bias_second_new, bias_new,
     ) = pl.pallas_call(
         finish,
         out_shape=shapes(handed_outs + own_outs),
-        in_specs=[in_vmem] * (5 + len(handed)),
-        out_specs=[in_vmem] * (5 + len(handed)),
+        in_specs=[in_vmem] * (8 + len(handed)),
+        out_specs=[in_vmem] * (8 + len(handed)),
         compiler_params=pltpu.CompilerParams(vmem_limit_bytes=64 * 2**20),
         name="finish",
-    )(rlay, rgrad, rest[8], norm_params, norm_second, *handed)
-
-    bias_grad = rest[9].reshape(NB_ROW)[:NB]
-    bias_second_new = 0.5 * bias_second + 0.5 * bias_grad * bias_grad
-    bias_new = biases - 0.5 * bias_grad * lax.rsqrt(bias_second_new + 1e-08)
+    )(rlay, rgrad, rest[8], rest[9], norm_params, norm_second, biases, bias_second, *handed)
+
     return (
         by_image(layer), by_image(gimg), gti.T, gto, gup.T, gdn, nti.T, nto, nup.T, ndn,
         lti, rti, lto, rto, lup, rup.T, ldn, rdn,

time: 157 us -> 139 us (0.89)
  Pallas kernels: 152 us -> 137 us
  local copies, waits for them, and re-layouts: 2.12 us -> 0 us
    pallas_call x1, Pallas kernels: 147 us -> 132 us  [on_device(): pl.pallas_call(fused, out_shape=shapes(outs), in_specs=[pl.BlockSpec(memo...]
where the time goes in v3:
time: 139 us; the launch traced here: 138 us
  Pallas kernels  137 us (99%)
  between operations  1.52 us (1%)
    pallas_call x1, Pallas kernels, on_device(): pl.pallas_call(fused, out_shape=shapes(outs), in_specs=[pl.BlockSpec(memo...  132 us
    pallas_call x1, Pallas kernels, on_device(): pl.pallas_call(finish, out_shape=shapes(handed_outs + own_outs), in_specs...  4.86 us

profile of v3, /device:TPU:1, one launch (start us, length us, event | category | flops | bytes accessed | tf_op | source)
XLA Modules:
  0.0 138.4 jit_solution(8657410881089278025)
XLA Ops:
  1.3 132.1 %fused.1 = (bf16[4,112,768]{2,1,0:T(8,128)(2,1)}, bf16[4,112,768]{2,1,0:T(8,128)(2,1)}, f32[12,768]{1,0:T(8,128)}, f32[12,768]{1,0:T(8,128)}, f32[12,768]{1,0:T(...) custom-call(s32[1]{0:T(128)S(6)} %copy.51.count, ...), custom_call_target="tpu_custom_call" | custom-call | tf_op jit(solution)/shard_map/fused/pallas_call | solution.py:890
  133.4 4.9 %finish.1 = (f32[12,768]{1,0:T(8,128)}, f32[12,768]{1,0:T(8,128)}, f32[12,768]{1,0:T(8,128)}, f32[12,768]{1,0:T(8,128)}, f32[12,3072]{1,0:T(8,128)}, /*index=5*/...) custom-call(bf16[4,112,768]{2,1,0:T(8,128)(2,1)} %get-tuple-element., ...), custom_call_target="tpu_custom_call" | custom-call | tf_op jit(solution)/shard_map/finish/pallas_call | solution.py:908

commit v4 on v3

--- a/solution.py
+++ b/solution.py
@@ -85,7 +85,7 @@
         ssem, rsem, lsem, stage, wst, tst, simg, scot, rimg, rcot,
         xw, W, tk, tokin, tokout, bti, bto, bup, brow, ximg, normed, mid, slope, act, n2, mb, br, dn,
         upc, dnc, actb, dpb, xbi, G, RAr, RAl, XA, YA, XB, YB, YC, XD, PZ, RZ,
-        HQ, UJQ, UJP, qst, Qx, XEo, XEi, SM, SB, SX, SZ, SY, SC, SF,
+        HQ, UJQ, UJP, qst, Qx, XEo, XEi, SM, SB, SX, SZ, S8, SF,
         cot, q_up, p_dn, old_r_up, old_l_dn, old_l_up, old_r_dn,
         pl_ti, pr_ti, pl_to, pr_to, ol_ti, or_ti, ol_to, or_to,
     ) = refs[NUM_LATE:]
@@ -145,7 +145,8 @@
         return value
 
     barrier = pltpu.get_barrier_semaphore()
-    peers = to_x[1:] + to_y[1:] + to_z[1:] + [sibling]
+    to_same = [dev(x, Y(i), z, cc) for i in range(NY) for cc in (c, 1 - c)][1:]
+    peers = to_x[1:] + to_z[1:] + to_same
     for peer in peers:
         pl.semaphore_signal(barrier, inc=1, device_id=peer, device_id_type=MESH)
 
@@ -225,8 +226,8 @@
     def c_ref(yy, zz):
         return W.at[yy, zz, rows_of(x), lanes_of(x, 2)]
 
-    def c_part(k, i):
-        return W.at[:, Z(k), rows_of(X(i)), lanes_of(X(i), 2)]
+    def c_part(k):
+        return W.at[:, Z(k), rows_of(x), lanes_of(x, 2)]
 
     W[y, z, rows_of(x), lanes_of(x, 2)] = upc[rows_of(x), lanes_of(x, 2)]
     own_a = W.at[y, z, :, P0]
@@ -264,7 +265,12 @@
         a_send(1, d, False)
     arrived(c_tz)
     c_ty = [put(tk.at[y, :, c], tk.at[y, :, c], to_y[i]) for i in range(1, NY)]
-    x_right, x_left, x_on, x_far = {}, {}, {}, []
+    c_x = {}
+
+    def x_send(k):
+        arrived(c_y[k])
+        c_x[k] = [put(c_part(k), c_part(k), to_x[i]) for i in range(1, NX)]
+
     for k in NEAR[1:]:
         c_z[NZ - k].wait_recv()
         c_send_y(k)
@@ -295,9 +301,7 @@
     arrived(c_ty)
     c_tc = put(tk.at[:, :, c], tk.at[:, :, c], sibling)
     for k in NEAR:
-        arrived(c_y[k])
-        x_right[k] = put(c_part(k, 0), c_part(k, 0), to_x[1])
-        x_left[k] = put(c_part(k, 0), c_part(k, 0), to_x[3])
+        x_send(k)
     for zz in range(NZ):
         for cc in range(2):
             first = [DS + S + 48 * ((yy * NZ + zz) * 2 + cc) for yy in range(NY)]
@@ -344,8 +348,7 @@
         normed[b] = (xhat * norm[0:1, :] + norm[1:2, :]).astype(BF)
     c_mb = put(mb.at[both], mb.at[both], sibling)
     for k in FAR:
-        arrived(c_y[k])
-        x_far += [put(c_part(k, 0), c_part(k, 0), to_x[i]) for i in range(1, NX)]
+        x_send(k)
     gather_step(2)
 
     @pl.loop(0, 2)
@@ -361,13 +364,6 @@
         n2[own_rows(b), :] = (xhat * norm[2:3, :] + norm[3:4, :]).astype(BF)
 
     c_n2 = put(n2.at[both], n2.at[both], sibling)
-    for k in NEAR:
-        if k < 2:
-            x_right[k].wait_recv()
-            x_on[k] = put(c_part(k, 3), c_part(k, 3), to_x[1])
-        else:
-            x_left[k].wait_recv()
-            x_on[k] = put(c_part(k, 1), c_part(k, 1), to_x[3])
     gather_step(3)
     gather_step(4)
     c_mb.wait_recv()
@@ -455,7 +451,7 @@
     for offset in (0, -1, 1, 2):
         arrived(b_y[offset])
     for k in NEAR:
-        arrived([x_left[k] if k < 2 else x_right[k], x_on[k]])
+        arrived(c_x[k])
     loads[0].wait()
     loads[1].wait()
     stage[0:12, :] = q_up[...]
@@ -474,7 +470,8 @@
     gradients(3)
     for offset in (-2, 3, -3, -4):
         arrived(b_y[offset])
-    arrived(x_far)
+    for k in FAR:
+        arrived(c_x[k])
     for d in (0, 1, 3, 2):
         (a_right if d < 2 else a_left)[4, d].wait_recv()
     channel_pass(0)
@@ -643,8 +640,8 @@
     own_out[1].start()
     c_grad = [put(scot.at[X(i)], rgrad.at[x], to_x[i]) for i in range(1, NX)]
     arrived(c_sz)
-    SY[y] = total(SB[x, z], *[SZ[i] for i in range(NZ - 1)]).astype(BF)
-    c_sy = [put(SY.at[y], SY.at[y], to_y[i]) for i in range(1, NY)]
+    S8[y, c] = total(SB[x, z], *[SZ[i] for i in range(NZ - 1)]).astype(BF)
+    c_s8 = [put(S8.at[y, c], S8.at[y, c], device) for device in to_same]
     for i in (1, 7, 2, 6):
         arrived(hz[i])
         h_spread(-i)
@@ -665,14 +662,12 @@
             j_copy(i).start()
         UJQ[...] = HQ[c, :, z]
 
-    arrived(c_sy)
-    SC[c] = total(SY[0], SY[1], SY[2], SY[3]).astype(BF)
-    c_sc = put(SC.at[c], SC.at[c], sibling)
     for i in (3, 5, 4):
         arrived(hz[i])
         h_spread(-i)
-    c_sc.wait_recv()
-    SF[x, z] = (total(SC[0], SC[1]) * PER_IMAGE).astype(BF)
+    arrived(c_s8)
+    parts = [S8[yy, cc] for yy in range(NY) for cc in range(2)]
+    SF[x, z] = (total(*parts) * PER_IMAGE).astype(BF)
     c_fz = [put(SF.at[x, z], SF.at[x, z], to_z[i]) for i in range(1, NZ)]
     for i in (1, 7, 2, 6):
         h_share(-i)
@@ -700,10 +695,10 @@
         UJP[u, 0:64] = dot(spread, upc[0:48, :]).astype(BF)
         UJP[u, 64:80] = channels
         out[...] = UJP[u, pl.ds(pl.multiple_of(16 * x, 16), 16), :][0:12].astype(F32)
+    for i in (3, 5, 4):
+        h_share(-i)
     arrived(c_fz)
     c_fx = [put(SF.at[x], SF.at[x], to_x[i]) for i in range(1, NX)]
-    for i in (3, 5, 4):
-        h_share(-i)
 
     arrived([hs[offset] for offset in (0, -1, -7, -2, -6, -3, -5, -4)])
     arrived(c_q)
@@ -880,7 +875,7 @@
         vm(BF, 2, 16, DC), vm(BF, 2, NX, 16, D),
         vm(BF, NX, 2, 16, 1792), vm(BF, NX, 2, 16, 1792),
         vm(F32, 512, DS), vm(BF, NY, NZ, 16, DS), vm(BF, 3, NZ, 16, DS), vm(BF, 7, 16, DS),
-        vm(BF, NY, 16, DS), vm(BF, 2, 16, DS), vm(BF, NY, NZ, 16, DS),
+        vm(BF, NY, 2, 16, DS), vm(BF, NY, NZ, 16, DS),
         vm(BF, patch_rows, D), vm(F32, 12, DC), vm(F32, 12, DC), vm(F32, 12, DC), vm(F32, 12, DC),
         vm(F32, 12, 192), vm(F32, 12, 192),
         *[vm(F32, n, n) for n in (S, DS, DS, S, S, DS, DS, S)],

time: 139 us -> 132 us (0.950)
  Pallas kernels: 137 us -> 130 us
    pallas_call x1, Pallas kernels: 132 us -> 125 us  [on_device(): pl.pallas_call(fused, out_shape=shapes(outs), in_specs=[pl.BlockSpec(memo...]
where the time goes in v4:
time: 132 us
  Pallas kernels  130 us (98%)
  between operations  1.52 us (1%)
    pallas_call x1, Pallas kernels, on_device(): pl.pallas_call(fused, out_shape=shapes(outs), in_specs=[pl.BlockSpec(memo...  125 us
    pallas_call x1, Pallas kernels, on_device(): pl.pallas_call(finish, out_shape=shapes(handed_outs + own_outs), in_specs...  4.86 us

profile of v4, /device:TPU:1, one launch (start us, length us, event | category | flops | bytes accessed | tf_op | source)
XLA Modules:
  0.0 131.7 jit_solution(1185261084547625195)
XLA Ops:
  1.3 125.3 %fused.1 = (bf16[4,112,768]{2,1,0:T(8,128)(2,1)}, bf16[4,112,768]{2,1,0:T(8,128)(2,1)}, f32[12,768]{1,0:T(8,128)}, f32[12,768]{1,0:T(8,128)}, f32[12,768]{1,0:T(...) custom-call(s32[1]{0:T(128)S(6)} %copy.51.count, ...), custom_call_target="tpu_custom_call" | custom-call | tf_op jit(solution)/shard_map/fused/pallas_call | solution.py:885
  126.6 4.9 %finish.1 = (f32[12,768]{1,0:T(8,128)}, f32[12,768]{1,0:T(8,128)}, f32[12,768]{1,0:T(8,128)}, f32[12,768]{1,0:T(8,128)}, f32[12,3072]{1,0:T(8,128)}, /*index=5*/...) custom-call(bf16[4,112,768]{2,1,0:T(8,128)(2,1)} %get-tuple-element., ...), custom_call_target="tpu_custom_call" | custom-call | tf_op jit(solution)/shard_map/finish/pallas_call | solution.py:903

commit v5 on v4

--- a/solution.py
+++ b/solution.py
@@ -76,7 +76,7 @@
 
 
 def fused(
-    count, img, cot_far, tin, tout, wup, wdn, norm, bias, *refs
+    count, img_far, cot_far, tin, tout, wup, wdn, norm, bias, *refs
 ):
     late = refs[:NUM_LATE]
     (
@@ -85,8 +85,8 @@
         ssem, rsem, lsem, stage, wst, tst, simg, scot, rimg, rcot,
         xw, W, tk, tokin, tokout, bti, bto, bup, brow, ximg, normed, mid, slope, act, n2, mb, br, dn,
         upc, dnc, actb, dpb, xbi, G, RAr, RAl, XA, YA, XB, YB, YC, XD, PZ, RZ,
-        HQ, UJQ, UJP, qst, Qx, XEo, XEi, SM, SB, SX, SZ, S8, SF,
-        cot, q_up, p_dn, old_r_up, old_l_dn, old_l_up, old_r_dn,
+        HQ, UJQ, UJP, qst, Qx, XEo, XEi, SM, SB, SY, SZ, S8, SF,
+        img, cot, q_up, p_dn, old_r_up, old_l_dn, old_l_up, old_r_dn,
         pl_ti, pr_ti, pl_to, pr_to, ol_ti, or_ti, ol_to, or_to,
     ) = refs[NUM_LATE:]
     loaded = (
@@ -145,11 +145,13 @@
         return value
 
     barrier = pltpu.get_barrier_semaphore()
-    to_same = [dev(x, Y(i), z, cc) for i in range(NY) for cc in (c, 1 - c)][1:]
-    peers = to_x[1:] + to_z[1:] + to_same
+    to_same = [dev(X(i), y, z, cc) for i in range(NX) for cc in (c, 1 - c)][1:]
+    peers = to_y[1:] + to_z[1:] + to_same
     for peer in peers:
         pl.semaphore_signal(barrier, inc=1, device_id=peer, device_id_type=MESH)
 
+    get_img = pltpu.make_async_copy(img_far, img, lsem.at[1])
+    get_img.start()
     get_cot = pltpu.make_async_copy(cot_far, cot, lsem.at[0])
     get_cot.start()
     loads = [None] * NUM_LATE
@@ -178,6 +180,7 @@
         return (col == (i - PATCHES * second) * 8 + 2 * m + second) & (i < 2 * PATCHES)
 
     chooser = pick(NX * PAIR, 8 * PATCHES, of_pairs)
+    get_img.wait()
     simg[...] = dot(chooser, img[...]).astype(BF).reshape(NX, PAIR, D)
     c_img = [put(simg.at[X(i)], rimg.at[x], to_x[i]) for i in range(1, NX)]
     get_cot.wait()
@@ -527,6 +530,9 @@
 
     a_reduce(3, (0, 1))
     to_patches(simg, c_img)
+    own_out = [pltpu.make_async_copy(simg.at[x], rlay.at[x], lsem.at[2])]
+    own_out[0].start()
+    c_lay = [put(simg.at[X(i)], rlay.at[x], to_x[i]) for i in range(1, NX)]
     a_reduce(3, (2, 3))
 
     roots = [
@@ -563,14 +569,15 @@
 
     second(3)
     second(6)
-    c_xa = []
-    for w in (1, 3, 2, 0):
+    for w in range(NX):
         ra[4, w].wait_recv()
         la[4, w].wait_recv()
         ref = G.at[X(w), z, :, P0]
         ref[...] = total(ref[...], RAr[3, w], RAl[3, w]).astype(BF)
-        if w > 0:
-            c_xa.append(put(ref, XA.at[w - 1], to_x[w]))
+    c_ya = [
+        put(G.at[:, z, rows_of(Y(i)), lanes_of(Y(i), 0)], YA.at[i - 1], to_y[i])
+        for i in range(1, NY)
+    ]
     for k in NEAR:
         third(k)
 
@@ -588,33 +595,32 @@
     for j, k in enumerate(FAR_FIRST):
         SM[pl.ds(464 + 8 * c + Z(k), 1), 0:192] = up_sums[:, 192 * j : 192 * j + 192]
     SB[...] = SM[...].reshape(NY, NZ, 16, DS).astype(BF)
-    c_sx = [put(SB.at[X(i)], SX.at[i - 1], to_x[i]) for i in range(1, NX)]
+    c_sy = [put(SB.at[Y(i)], SY.at[i - 1], to_y[i]) for i in range(1, NY)]
 
     for k in (4, 5):
         third(k)
-    arrived(c_xa)
-    ref = G.at[x, z, :, P0]
-    ref[...] = total(ref[...], XA[0], XA[1], XA[2]).astype(BF)
-    c_ya = [
-        put(G.at[x, z, rows_of(Y(i)), lanes_of(Y(i), 0)], YA.at[i - 1], to_y[i])
-        for i in range(1, NY)
+    arrived(c_ya)
+    ref = G.at[:, z, rows_of(y), lanes_of(y, 0)]
+    ref[...] = total(ref[...], YA[0], YA[1], YA[2]).astype(BF)
+    c_xa = [
+        put(G.at[X(i), z, rows_of(y), lanes_of(y, 0)], XA.at[i - 1], to_x[i]) for i in range(1, NX)
     ]
     for k in (3, 6):
         third(k)
-    arrived(c_sx)
-    SB[x] = total(SB[x], SX[0], SX[1], SX[2]).astype(BF)
-    c_sz = [put(SB.at[x, Z(i)], SZ.at[i - 1], to_z[i]) for i in range(1, NZ)]
+    arrived(c_sy)
+    SB[y] = total(SB[y], SY[0], SY[1], SY[2]).astype(BF)
+    c_sz = [put(SB.at[y, Z(i)], SZ.at[i - 1], to_z[i]) for i in range(1, NZ)]
 
 
     hz, hy, hs = {}, {}, {}
 
     def h_send(lanes):
         ref = HQ.at[c, y, z, :, lanes]
-        for i in (4, 3, 5, 2, 6, 1, 7):
+        for i in (1, 7, 2, 6, 3, 5, 4):
             hz[i] = hz.get(i, []) + [put(ref, ref, to_z[i])]
 
-    arrived(c_ya)
-    mean = total(G[x, z, rows_of(y), lanes_of(y, 0)], YA[0], YA[1], YA[2]) * PER_IMAGE
+    arrived(c_xa)
+    mean = total(G[x, z, rows_of(y), lanes_of(y, 0)], XA[0], XA[1], XA[2]) * PER_IMAGE
     HQ[c, y, z, :, 0:TILE] = mean.astype(BF)
     h_send(slice(0, TILE))
     arrived(rz.values())
@@ -632,16 +638,13 @@
         hs[offset] = put(ref, ref, sibling)
 
     h_spread(0)
-    own_out = [pltpu.make_async_copy(simg.at[x], rlay.at[x], lsem.at[2])]
-    own_out[0].start()
-    c_lay = [put(simg.at[X(i)], rlay.at[x], to_x[i]) for i in range(1, NX)]
     to_patches(scot, c_cot)
     own_out.append(pltpu.make_async_copy(scot.at[x], rgrad.at[x], lsem.at[3]))
     own_out[1].start()
     c_grad = [put(scot.at[X(i)], rgrad.at[x], to_x[i]) for i in range(1, NX)]
     arrived(c_sz)
-    S8[y, c] = total(SB[x, z], *[SZ[i] for i in range(NZ - 1)]).astype(BF)
-    c_s8 = [put(S8.at[y, c], S8.at[y, c], device) for device in to_same]
+    S8[x, c] = total(SB[y, z], *[SZ[i] for i in range(NZ - 1)]).astype(BF)
+    c_s8 = [put(S8.at[x, c], S8.at[x, c], device) for device in to_same]
     for i in (1, 7, 2, 6):
         arrived(hz[i])
         h_spread(-i)
@@ -666,9 +669,9 @@
         arrived(hz[i])
         h_spread(-i)
     arrived(c_s8)
-    parts = [S8[yy, cc] for yy in range(NY) for cc in range(2)]
-    SF[x, z] = (total(*parts) * PER_IMAGE).astype(BF)
-    c_fz = [put(SF.at[x, z], SF.at[x, z], to_z[i]) for i in range(1, NZ)]
+    parts = [S8[xx, cc] for xx in range(NX) for cc in range(2)]
+    SF[y, z] = (total(*parts) * PER_IMAGE).astype(BF)
+    c_fz = [put(SF.at[y, z], SF.at[y, z], to_z[i]) for i in range(1, NZ)]
     for i in (1, 7, 2, 6):
         h_share(-i)
     @pl.when(x != y)
@@ -698,7 +701,7 @@
     for i in (3, 5, 4):
         h_share(-i)
     arrived(c_fz)
-    c_fx = [put(SF.at[x], SF.at[x], to_x[i]) for i in range(1, NX)]
+    c_fy = [put(SF.at[y], SF.at[y], to_y[i]) for i in range(1, NY)]
 
     arrived([hs[offset] for offset in (0, -1, -7, -2, -6, -3, -5, -4)])
     arrived(c_q)
@@ -724,7 +727,7 @@
     for copy in loads[4:]:
         copy.wait()
 
-    arrived(c_fx)
+    arrived(c_fy)
     small = SF[...].reshape(512, DS)
     o_norm[...] = small[208:216].astype(F32)
     vector = small[208:256].astype(F32)
@@ -868,15 +871,15 @@
         vm(BF, D, D), vm(BF, D, D), vm(BF, 4 * ROW, 2 * D), vm(BF, 4 * ROW, 2 * D),
         vm(BF, 2, 2 * ROW, D),
         vm(BF, NY, NZ, 96, D),
-        vm(BF, 4, NX, 96, 256), vm(BF, 4, NX, 96, 256), vm(BF, 3, 96, 256), vm(BF, 3, 48, TILE),
+        vm(BF, 4, NX, 96, 256), vm(BF, 4, NX, 96, 256), vm(BF, 3, 48, TILE), vm(BF, 3, NX, 48, TILE),
         vm(BF, 3, NZ, 96, 256), vm(BF, 3, NZ, NY, 48, TILE), vm(BF, 3, NZ, 48, TILE), vm(BF, 3, NZ, 48, TILE),
         vm(BF, NZ, 48, 256), vm(BF, 7, 48, 256),
         vm(BF, 2, NY, NZ, 48, DS), vm(BF, NY, 48, DS), vm(BF, 2, 80, D),
         vm(BF, 2, 16, DC), vm(BF, 2, NX, 16, D),
         vm(BF, NX, 2, 16, 1792), vm(BF, NX, 2, 16, 1792),
         vm(F32, 512, DS), vm(BF, NY, NZ, 16, DS), vm(BF, 3, NZ, 16, DS), vm(BF, 7, 16, DS),
-        vm(BF, NY, 2, 16, DS), vm(BF, NY, NZ, 16, DS),
-        vm(BF, patch_rows, D), vm(F32, 12, DC), vm(F32, 12, DC), vm(F32, 12, DC), vm(F32, 12, DC),
+        vm(BF, NX, 2, 16, DS), vm(BF, NY, NZ, 16, DS),
+        vm(BF, patch_rows, D), vm(BF, patch_rows, D), vm(F32, 12, DC), vm(F32, 12, DC), vm(F32, 12, DC), vm(F32, 12, DC),
         vm(F32, 12, 192), vm(F32, 12, 192),
         *[vm(F32, n, n) for n in (S, DS, DS, S, S, DS, DS, S)],
     ]
@@ -886,7 +889,7 @@
         fused,
         out_shape=shapes(outs),
         in_specs=[pl.BlockSpec(memory_space=pltpu.SMEM)]
-        + [anywhere if i == 2 or i > 8 else in_vmem for i in range(1, len(args))],
+        + [anywhere if i < 3 or i > 8 else in_vmem for i in range(1, len(args))],
         out_specs=[anywhere, anywhere] + [in_vmem] * (len(outs) - 2),
         scratch_shapes=scratch,
         compiler_params=pltpu.CompilerParams(

time: 132 us -> 129 us (0.977)
  Pallas kernels: 130 us -> 126 us
    pallas_call x1, Pallas kernels: 125 us -> 121 us  [on_device(): pl.pallas_call(fused, out_shape=shapes(outs), in_specs=[pl.BlockSpec(memo...]
where the time goes in v5:
time: 129 us; the launch traced here: 128 us
  Pallas kernels  126 us (98%)
  between operations  1.52 us (1%)
    pallas_call x1, Pallas kernels, on_device(): pl.pallas_call(fused, out_shape=shapes(outs), in_specs=[pl.BlockSpec(memo...  121 us
    pallas_call x1, Pallas kernels, on_device(): pl.pallas_call(finish, out_shape=shapes(handed_outs + own_outs), in_specs...  4.87 us

profile of v5, /device:TPU:1, one launch (start us, length us, event | category | flops | bytes accessed | tf_op | source)
XLA Modules:
  0.0 127.6 jit_solution(4872994115620958772)
XLA Ops:
  1.3 121.2 %fused.1 = (bf16[4,112,768]{2,1,0:T(8,128)(2,1)}, bf16[4,112,768]{2,1,0:T(8,128)(2,1)}, f32[12,768]{1,0:T(8,128)}, f32[12,768]{1,0:T(8,128)}, f32[12,768]{1,0:T(...) custom-call(s32[1]{0:T(128)S(6)} %copy.51.count, ...), custom_call_target="tpu_custom_call" | custom-call | tf_op jit(solution)/shard_map/fused/pallas_call | solution.py:888
  122.5 4.9 %finish.1 = (f32[12,768]{1,0:T(8,128)}, f32[12,768]{1,0:T(8,128)}, f32[12,768]{1,0:T(8,128)}, f32[12,768]{1,0:T(8,128)}, f32[12,3072]{1,0:T(8,128)}, /*index=5*/...) custom-call(bf16[4,112,768]{2,1,0:T(8,128)(2,1)} %get-tuple-element., ...), custom_call_target="tpu_custom_call" | custom-call | tf_op jit(solution)/shard_map/finish/pallas_call | solution.py:906

commit v6 on v5

--- a/solution.py
+++ b/solution.py
@@ -622,11 +622,10 @@
     arrived(c_xa)
     mean = total(G[x, z, rows_of(y), lanes_of(y, 0)], XA[0], XA[1], XA[2]) * PER_IMAGE
     HQ[c, y, z, :, 0:TILE] = mean.astype(BF)
-    h_send(slice(0, TILE))
     arrived(rz.values())
     mean = total(PZ[z], *[RZ[i] for i in range(NZ - 1)]) * PER_IMAGE
     HQ[c, y, z, :, TILE:] = mean.astype(BF)
-    h_send(slice(TILE, DS))
+    h_send(slice(0, DS))
 
     def h_spread(offset):
         ref = HQ.at[c, y, Z(offset)]

time: 129 us -> 130 us (level)
  Pallas kernels: 126 us -> 128 us
    pallas_call x1, Pallas kernels: 121 us -> 123 us  [on_device(): pl.pallas_call(fused, out_shape=shapes(outs), in_specs=[pl.BlockSpec(memo...]
where the time goes in v6:
time: 130 us; the launch traced here: 129 us
  Pallas kernels  128 us (98%)
  between operations  1.52 us (1%)
    pallas_call x1, Pallas kernels, on_device(): pl.pallas_call(fused, out_shape=shapes(outs), in_specs=[pl.BlockSpec(memo...  123 us
    pallas_call x1, Pallas kernels, on_device(): pl.pallas_call(finish, out_shape=shapes(handed_outs + own_outs), in_specs...  4.86 us

profile of v6, /device:TPU:1, one launch (start us, length us, event | category | flops | bytes accessed | tf_op | source)
XLA Modules:
  0.0 129.4 jit_solution(5205577458656127475)
XLA Ops:
  1.3 123.0 %fused.1 = (bf16[4,112,768]{2,1,0:T(8,128)(2,1)}, bf16[4,112,768]{2,1,0:T(8,128)(2,1)}, f32[12,768]{1,0:T(8,128)}, f32[12,768]{1,0:T(8,128)}, f32[12,768]{1,0:T(...) custom-call(s32[1]{0:T(128)S(6)} %copy.51.count, ...), custom_call_target="tpu_custom_call" | custom-call | tf_op jit(solution)/shard_map/fused/pallas_call | solution.py:887
  124.3 4.9 %finish.1 = (f32[12,768]{1,0:T(8,128)}, f32[12,768]{1,0:T(8,128)}, f32[12,768]{1,0:T(8,128)}, f32[12,768]{1,0:T(8,128)}, f32[12,3072]{1,0:T(8,128)}, /*index=5*/...) custom-call(bf16[4,112,768]{2,1,0:T(8,128)(2,1)} %get-tuple-element., ...), custom_call_target="tpu_custom_call" | custom-call | tf_op jit(solution)/shard_map/finish/pallas_call | solution.py:905
